TPU v7x, 32 devices: a whole 2x2x4 slice. The times are simulated.
32 devices in a mesh: groups: 2 (over x), expert: 8 (over z, y), dp: 2 (over core).
Axes of the slice: x: 2, y: 2, z: 4, core: 2. Of those that a mesh axis runs over, the one named last changes fastest.
Arguments:
- tokens: bfloat16 [2048, 7168], P(('groups', 'expert', 'dp')), parts along dimension 0, may hold values from -6 to 6
- expert_ids: int32 [2048, 2], P(('groups', 'expert', 'dp')), parts along dimension 0, may hold values from 0 to 3, all different within a row; in each aligned block of 64 rows (0 to 63, 64 to 127, ...) at most 40 rows name the same one
- router_values: float32 [2048, 2], P(('groups', 'expert', 'dp')), parts along dimension 0, may hold values from 0.1 to 1
- gate_weight: bfloat16 [7168, 4096], P(None, ('expert', 'dp')), may hold values from -0.0625 to 0.0625
- up_weight: bfloat16 [7168, 4096], P(None, ('expert', 'dp')), may hold values from -0.0625 to 0.0625
- down_weight: bfloat16 [4096, 7168], P(('expert', 'dp')), may hold values from -0.1875 to 0.1875
Outputs:
- routed_out: bfloat16 [2048, 7168], P(('groups', 'expert', 'dp')), parts along dimension 0
There are 2 independent parts, one for each index of `groups`. A program takes and returns all parts, laid end to end along the dimension named above; an argument that names none is the same for every part. Nothing has to cross between parts.
Inputs may be any that keep to these rules, and one draw needn't show every extreme that they name: `expert_ids`: each row names 2 different experts. Among the tokens of one device (aligned blocks of 64 rows) no expert is named more than 40 times, and in every draw some expert is named exactly 40 times in some device's tokens.
All inputs are finite; a program needn't handle non-finite values.
Results may differ from a plain program's by a relative error of at most 0.02.
Values may be sent and summed in bfloat16 or wider, within the bound.
No kernel may reach another device: no remote copies, remote signals or barrier semaphores. Data moves between devices by JAX's collectives and lax.ppermute only.
A program may use at most 192 MiB of HBM per device.

v0:
```python
import jax
import jax.numpy as jnp
from jax import lax
from jax.sharding import PartitionSpec as P

SLICES = 4


def expert_block(arrived, arrived_scales, gate_weight, up_weight, down_weight):
    slot_groups, slot_count, feature_width = arrived.shape
    blocks = arrived_scales.shape[2]
    grouped = arrived.astype(jnp.float32).reshape(slot_groups, slot_count, blocks, 128)
    restored = (grouped * arrived_scales.astype(jnp.float32)[:, :, :, None]).astype(jnp.bfloat16)
    flat_rows = restored.reshape(slot_groups * slot_count, feature_width)
    gate_value = jnp.dot(flat_rows, gate_weight, preferred_element_type=jnp.float32)
    up_value = jnp.dot(flat_rows, up_weight, preferred_element_type=jnp.float32)
    hidden = (jax.nn.silu(gate_value) * up_value).astype(jnp.bfloat16)
    result = jnp.dot(hidden, down_weight, preferred_element_type=jnp.float32).astype(jnp.bfloat16)
    return result.reshape(slot_groups, slot_count, feature_width)


def local(tokens, expert_ids, router_values, gate_weight, up_weight, down_weight):
    row_count, feature_width = tokens.shape
    route_count = expert_ids.shape[1]
    replica_count = lax.axis_size("dp")
    expert_rows = lax.axis_size("expert")
    device_count = expert_rows * replica_count
    expert_count = device_count // SLICES
    capacity = row_count * route_count // expert_count * 5 // 4
    blocks = feature_width // 128
    combine = 2.5 * router_values / jnp.sum(router_values, axis=1, keepdims=True)
    grouped = tokens.astype(jnp.float32).reshape(row_count, blocks, 128)
    block_scale = (jnp.max(jnp.abs(grouped), axis=2) / 448.0 + 1e-06).astype(jnp.bfloat16)
    quantized = (
        (grouped / block_scale.astype(jnp.float32)[:, :, None])
        .astype(jnp.bfloat16)
        .reshape(row_count, feature_width)
    )
    chosen = expert_ids.reshape(row_count * route_count)
    member = (chosen[:, None] == jnp.arange(expert_count, dtype=jnp.int32)[None, :]).astype(
        jnp.int32
    )
    earlier = jnp.cumsum(member, axis=0) - member
    position = jnp.sum(earlier * member, axis=1)
    slot_index = chosen * capacity + position
    pair_table = (
        slot_index[:, None] == jnp.arange(expert_count * capacity, dtype=jnp.int32)[None, :]
    ).astype(jnp.float32)
    selection = jnp.sum(pair_table.reshape(row_count, route_count, expert_count * capacity), axis=1)
    placer = selection.T.astype(jnp.bfloat16)
    send_rows = (
        jnp.dot(placer, quantized, preferred_element_type=jnp.float32)
        .astype(jnp.bfloat16)
        .reshape(expert_count, capacity, feature_width)
    )
    send_scales = (
        jnp.dot(placer, block_scale, preferred_element_type=jnp.float32)
        .astype(jnp.bfloat16)
        .reshape(expert_count, capacity, blocks)
    )
    per_index = SLICES // replica_count
    copy_rows = jnp.broadcast_to(
        send_rows[:, None], (expert_count, per_index, capacity, feature_width)
    ).reshape(expert_rows, capacity, feature_width)
    copy_scales = jnp.broadcast_to(
        send_scales[:, None], (expert_count, per_index, capacity, blocks)
    ).reshape(expert_rows, capacity, blocks)
    own_rows, own_scales = (
        lax.all_to_all(copy_rows, "expert", split_axis=0, concat_axis=0, tiled=True),
        lax.all_to_all(copy_scales, "expert", split_axis=0, concat_axis=0, tiled=True),
    )
    both_rows, both_scales = (
        lax.all_gather(own_rows, "dp", axis=0, tiled=True),
        lax.all_gather(own_scales, "dp", axis=0, tiled=True),
    )
    produced = expert_block(both_rows, both_scales, gate_weight, up_weight, down_weight)
    produced = produced.reshape(replica_count, expert_rows, capacity, feature_width)
    returned = lax.all_to_all(
        lax.all_to_all(produced, "expert", split_axis=1, concat_axis=1, tiled=True),
        "dp",
        split_axis=0,
        concat_axis=0,
        tiled=True,
    )
    pair_out = jnp.sum(returned.astype(jnp.float32), axis=0).astype(jnp.bfloat16)
    gathered = jnp.sum(
        pair_out.astype(jnp.float32).reshape(expert_count, per_index, capacity, feature_width),
        axis=1,
    )
    flat_gathered = gathered.reshape(expert_count * capacity, feature_width)
    picked = jnp.take(flat_gathered, slot_index, axis=0)
    weighted = picked * combine.reshape(row_count * route_count, 1)
    routed_out = jnp.sum(weighted.reshape(row_count, route_count, feature_width), axis=1)
    return routed_out.astype(jnp.bfloat16)


def solution(mesh):
    in_specs = (
        P(("groups", "expert", "dp"), None),
        P(("groups", "expert", "dp"), None),
        P(("groups", "expert", "dp"), None),
        P(None, ("expert", "dp")),
        P(None, ("expert", "dp")),
        P(("expert", "dp"), None),
    )
    out_specs = P(("groups", "expert", "dp"), None)
    return jax.shard_map(local, mesh=mesh, in_specs=in_specs, out_specs=out_specs, check_vma=False)
```

profile of v0, /device:TPU:0, one launch (start us, length us, event | category | flops | bytes accessed | tf_op | source)
XLA Modules:
  0.0 464.9 jit_solution(10184768032523986383)
XLA Ops:
  6.5 0.8 copy.33
  8.1 0.7 compare_and_fusion
  8.9 1.3 fusion.1
  10.6 0.5 reduce_max.9
  11.7 0.8 convolution_convert_fusion.1
  13.0 109.2 %all_to_all.20 = bf16[8,40,7168]{2,1,0:T(8,128)(2,1)} all-to-all(bf16[8,40,7168]{2,1,0:T(8,128)(2,1)S(1)} %bitcast.50), channel_id=1, replica_groups=mesh['groups'=2,'expert'=8,'dp'=2] {'expert'}, dimensions={0} | all-to-all | bytes 9175040 | tf_op jit(solution)/shard_map/all_to_all | solution.py:69
  122.7 9.7 %all_to_all.21 = bf16[8,2,1120]{2,1,0:T(2,128)(2,1)S(1)} all-to-all(bf16[8,2,1120]{2,1,0:T(2,128)(2,1)S(1)} %reshape.120), channel_id=1, replica_groups=mesh['groups'=2,'expert'=8,'dp'=2] {'expert'}, dimensions={0} | all-to-all | bytes 71680 | tf_op jit(solution)/shard_map/all_to_all | solution.py:70
  132.6 2.1 all_gather.7
  134.7 7.9 %all-gather.2.cloned.1.call-done = bf16[16,40,7168]{2,1,0:T(8,128)(2,1)} async-done(((bf16[8,40,7168]{2,1,0:T(8,128)(2,1)}), bf16[16,40,7168]{2,1,0:T(8,128)(2,1)}) %all-gather.2.cloned.1.call-update) | async-done | bytes 9175056 | tf_op jit(solution)/shard_map/all_gather | solution.py:73
  142.6 5.1 %mul.61 = f32[16,40,56,128]{3,2,1,0:T(8,128)S(1)} broadcast(bf16[16,40,56]{2,1,0:T(8,128)(2,1)S(1)} %all_gather.7), dimensions={0,1,2} | broadcast | bytes 18421760 | tf_op jit(solution)/shard_map/mul | solution.py:13
  147.6 4.5 fusion
  152.1 3.5 copy-done
  155.7 4.6 fusion.14
  160.3 18.9 %convolution_convert_fusion = bf16[640,7168]{1,0:T(8,128)(2,1)} fusion(bf16[256,7168]{1,0:T(8,128)(2,1)} %param.11, bf16[640,7168]{1,0:T(8,128)(2,1)} %copy-done, bf16[7168,256]{1,0:T(8,128)(2,1)} %param.10, f32[640,256]{1,0:T(8,128)S(1)} %fusion.14), kind=kOutput, calls=%fused_computation.3 | convolution fusion | flops 4703191040 | bytes 26345472 | tf_op jit(solution)/shard_map/dot_general | solution.py:18
  179.1 8.0 %copy.37 = bf16[2,8,40,7168]{3,2,0,1:T(8,128)(2,1)} copy(bf16[2,8,40,7168]{3,2,1,0:T(8,128)(2,1)} %bitcast.49) | data formatting | bytes 18350080 | tf_op jit(solution)/shard_map/reshape;reshape | solution.py:77
  187.1 5.9 %all-to-all-start.2 = ((bf16[2,8,40,7168]{3,2,0,1:T(8,128)(2,1)}), bf16[2,8,40,7168]{3,2,0,1:T(8,128)(2,1)}, u32[]{:S(2)}, u32[]{:S(2)}) async-start(bf16[2,8,40,7168]{3,2,0,1:T(8,128)(2,1)} %copy.37), calls=%async_computation.2 | async-start | bytes 18350080 | tf_op jit(solution)/shard_map/all_to_all | solution.py:79
  193.6 200.0 %all-to-all-done.2 = bf16[2,8,40,7168]{3,2,0,1:T(8,128)(2,1)} async-done(((bf16[2,8,40,7168]{3,2,0,1:T(8,128)(2,1)}), bf16[2,8,40,7168]{3,2,0,1:T(8,128)(2,1)}, u32[]{:S(2)}, u32[]{:S(2)}) %all-to-all-start.2) | async-done | bytes 9175072 | tf_op jit(solution)/shard_map/all_to_all | solution.py:79
  393.5 7.9 %copy.38 = bf16[2,8,40,7168]{3,2,1,0:T(8,128)(2,1)} copy(bf16[2,8,40,7168]{3,2,0,1:T(8,128)(2,1)} %all-to-all-done.2) | data formatting | bytes 18350080 | tf_op jit(solution)/shard_map/all_to_all | solution.py:79
  401.4 19.8 %all_to_all.22 = bf16[2,8,40,7168]{3,2,1,0:T(8,128)(2,1)} all-to-all(bf16[2,8,40,7168]{3,2,1,0:T(8,128)(2,1)} %copy.38), channel_id=1, replica_groups=mesh['groups'=2,'expert'=8,'dp'=2] {'dp'}, dimensions={0} | all-to-all | bytes 18350080 | tf_op jit(solution)/shard_map/all_to_all | solution.py:78
  421.2 9.0 %reduce_sum.64 = bf16[8,40,7168]{2,1,0:T(8,128)(2,1)} reduce(bf16[2,8,40,7168]{3,2,1,0:T(8,128)(2,1)} %all_to_all.22, bf16[]{:T(256)} %constant.36.clone.1), dimensions={0}, to_apply=%region_4.5 | reduce | flops 2293760 | bytes 13762562 | tf_op jit(solution)/shard_map/reduce_sum | solution.py:85
  430.2 5.8 %convert_reduce_fusion = f32[4,40,7168]{2,1,0:T(8,128)} fusion(bf16[8,40,7168]{2,1,0:T(8,128)(2,1)} %reduce_sum.64), kind=kLoop, calls=%fused_computation.4 | loop fusion | flops 3440640 | bytes 9175040 | tf_op jit(solution)/shard_map/reduce_sum | solution.py:86
  436.0 7.3 %gather_fusion = f32[128,7168]{1,0:T(8,128)} fusion(f32[160,7168]{1,0:T(8,128)} %bitcast.47, s32[1024]{0:T(1024)S(1)} %pad_clamp_fusion), kind=kCustom, calls=%fused_computation | custom fusion | bytes 7340544 | tf_op jit(solution)/shard_map/jit(_take)/gather | solution.py:91
  443.3 5.5 %gather.7 = f32[64,2,7168]{2,1,0:T(2,128)} reshape(f32[128,7168]{1,0:T(8,128)} %gather_fusion) | data formatting | bytes 7340032 | tf_op jit(solution)/shard_map/jit(_take)/gather | solution.py:91
  448.8 9.3 %multiply_reduce_fusion = bf16[64,7168]{1,0:T(8,128)(2,1)} fusion(f32[64,2,7168]{2,1,0:T(2,128)} %gather.7, pred[64,2]{1,0:T(8,128)(4,1)S(1)} %copy.35, f32[64,2]{1,0:T(8,128)S(1)} %copy.40), kind=kLoop, calls=%fused_computation.6 | loop fusion | flops 2293760 | bytes 4588160 | tf_op jit(solution)/shard_map/reduce_sum | solution.py:93
  (36 shorter events, 3.4 us)
Async XLA Ops:
  6.5 136.0 %all-gather.2.cloned.1.call-start = ((), (), s32[]{:S(2)}) async-start(), calls=%async_computation.4 | async-start | bytes 13762560 | tf_op jit(solution)/shard_map/all_gather | solution.py:73
  10.2 1.4 copy-start.2
  142.6 5.1 %copy-start.1 = (bf16[16,40,7168]{2,1,0:T(8,128)(2,1)S(1)}, bf16[16,40,7168]{2,1,0:T(8,128)(2,1)}, u32[]{:S(2)}) copy-start(bf16[16,40,7168]{2,1,0:T(8,128)(2,1)} %all-gather.2.cloned.1.call-done) | copy-start | bytes 27525124
  152.1 3.6 copy-start
  187.1 5.9 %copy-start.3 = (s32[64,2]{0,1:T(2,128)S(1)}, s32[64,2]{0,1:T(2,128)}, u32[]{:S(2)}) copy-start(s32[64,2]{0,1:T(2,128)} %param.7) | copy-start | bytes 1540
  187.1 6.3 %copy-start.4 = (f32[64,2]{0,1:T(2,128)S(1)}, f32[64,2]{0,1:T(2,128)}, u32[]{:S(2)}) copy-start(f32[64,2]{0,1:T(2,128)} %param.8) | copy-start | bytes 1540
  187.1 206.4 %all-to-all-start.2 = ((bf16[2,8,40,7168]{3,2,0,1:T(8,128)(2,1)}), bf16[2,8,40,7168]{3,2,0,1:T(8,128)(2,1)}, u32[]{:S(2)}, u32[]{:S(2)}) async-start(bf16[2,8,40,7168]{3,2,0,1:T(8,128)(2,1)} %copy.37), calls=%async_computation.2 | async-start | bytes 18350080 | tf_op jit(solution)/shard_map/all_to_all | solution.py:79
Sparse Core Ops, SparseCore 0:
  122.3 20.1 all-gather.1
where the time goes:
time: 466 us; the launch traced here: 465 us
  waiting for transfers between devices  208 us (45%)
  blocking collectives  141 us (30%)
  local copies, waits for them, and re-layouts  40.7 us (9%)
  other arithmetic  31.6 us (7%)
  matrix products  24.4 us (5%)
  between operations  13.6 us (3%)
  starting transfers between devices  5.91 us (1%)
    all_to_all x1, waiting for transfers between devices, local(): lax.all_to_all(produced, 'expert', split_axis=1, concat_axis=1, tiled=True)  200 us
    all_to_all x1, blocking collectives, local(): lax.all_to_all(copy_rows, 'expert', split_axis=0, concat_axis=0, tiled=True)  109 us
    all_to_all x1, blocking collectives, local(): lax.all_to_all(lax.all_to_all(produced, 'expert', split_axis=1, concat_ax...  19.8 us
    dot_general x1, matrix products, expert_block(): jnp.dot(hidden, down_weight, preferred_element_type=jnp.float32)  18.9 us
    gather x2, local copies, waits for them, and re-layouts, local(): picked = jnp.take(flat_gathered, slot_index, axis=0)  12.8 us
    all_to_all x1, blocking collectives, local(): lax.all_to_all(copy_scales, 'expert', split_axis=0, concat_axis=0, tiled=...  9.74 us
  transfers between devices with their start and end apart: 2, of which 2 were waited for; matrix products, arithmetic and copies ran while one was open for 0% of the time, Pallas kernels for 0%

commit v1 on v0

v1 whole, which is shorter than its diff:
```python
import jax
import jax.numpy as jnp
from jax import lax
from jax.sharding import PartitionSpec as P

SLICES = 4


def expert_rows_of(tokens):
    row_count, feature_width = tokens.shape
    grouped = tokens.astype(jnp.float32).reshape(row_count, feature_width // 128, 128)
    scale = (jnp.max(jnp.abs(grouped), axis=2) / 448.0 + 1e-06).astype(jnp.bfloat16)
    wide = scale.astype(jnp.float32)[:, :, None]
    quantized = (grouped / wide).astype(jnp.bfloat16)
    restored = (quantized.astype(jnp.float32) * wide).astype(jnp.bfloat16)
    return restored.reshape(row_count, feature_width)


def expert_block(rows, gate_weight, up_weight, down_weight):
    gate_value = jnp.dot(rows, gate_weight, preferred_element_type=jnp.float32)
    up_value = jnp.dot(rows, up_weight, preferred_element_type=jnp.float32)
    hidden = (jax.nn.silu(gate_value) * up_value).astype(jnp.bfloat16)
    return jnp.dot(hidden, down_weight, preferred_element_type=jnp.float32).astype(jnp.bfloat16)


def add_rows(left, right):
    return (left.astype(jnp.float32) + right.astype(jnp.float32)).astype(jnp.bfloat16)


def local(tokens, expert_ids, router_values, gate_weight, up_weight, down_weight):
    row_count, _ = tokens.shape
    route_count = expert_ids.shape[1]
    replicas = lax.axis_size("dp")
    chips = lax.axis_size("expert")
    experts = chips * replicas // SLICES
    per = chips // experts
    capacity = row_count * route_count // experts * 5 // 4
    slots = experts * capacity
    assert replicas == 2 and per == 2

    home = lax.axis_index("expert") // per
    across = [(i, i ^ 1) for i in range(chips)]
    cores = [(0, 1), (1, 0)]

    def shifted(step):
        return [(i, (i + per * step) % chips) for i in range(chips)]

    combine = 2.5 * router_values / jnp.sum(router_values, axis=1, keepdims=True)
    chosen = lax.rem(expert_ids - home + experts, experts).reshape(row_count * route_count)
    member = (chosen[:, None] == jnp.arange(experts, dtype=jnp.int32)[None, :]).astype(jnp.int32)
    earlier = jnp.cumsum(member, axis=0) - member
    position = jnp.sum(earlier * member, axis=1)
    slot_index = (chosen * capacity + position).reshape(row_count, route_count)
    pair_table = slot_index[:, :, None] == jnp.arange(slots, dtype=jnp.int32)[None, None, :]
    placer = jnp.any(pair_table, axis=1).astype(jnp.bfloat16)
    weights = jnp.sum(jnp.where(pair_table, combine[:, :, None], 0.0), axis=1)
    weights_high = lax.reduce_precision(weights, 8, 7)
    weights_low = weights - weights_high
    both_weights = jnp.concatenate([weights_high, weights_low], axis=0).astype(jnp.bfloat16)

    rows = expert_rows_of(tokens)
    send = lax.dot_general(
        placer, rows, (((0,), (0,)), ((), ())), preferred_element_type=jnp.float32
    ).astype(jnp.bfloat16)

    returned = []
    for step in range(experts):
        own = send[step * capacity : (step + 1) * capacity]
        if step:
            own = lax.ppermute(own, "expert", shifted(step))
        other = lax.ppermute(own, "expert", across)
        pair = jnp.concatenate([own, other], axis=0)
        far = lax.ppermute(pair, "dp", cores)
        produced = expert_block(
            jnp.concatenate([pair, far], axis=0), gate_weight, up_weight, down_weight
        )
        half = add_rows(
            produced[: 2 * capacity], lax.ppermute(produced[2 * capacity :], "dp", cores)
        )
        whole = add_rows(half[:capacity], lax.ppermute(half[capacity:], "expert", across))
        if step:
            whole = lax.ppermute(whole, "expert", shifted(experts - step))
        returned.append(whole)
    product = jnp.dot(
        both_weights, jnp.concatenate(returned, axis=0), preferred_element_type=jnp.float32
    )
    return (product[:row_count] + product[row_count:]).astype(jnp.bfloat16)


def solution(mesh):
    in_specs = (
        P(("groups", "expert", "dp"), None),
        P(("groups", "expert", "dp"), None),
        P(("groups", "expert", "dp"), None),
        P(None, ("expert", "dp")),
        P(None, ("expert", "dp")),
        P(("expert", "dp"), None),
    )
    out_specs = P(("groups", "expert", "dp"), None)
    return jax.shard_map(local, mesh=mesh, in_specs=in_specs, out_specs=out_specs, check_vma=False)
```

time: 466 us -> 229 us (0.49)
  blocking collectives: 141 us -> 0 us
  waiting for transfers between devices: 208 us -> 133 us
  local copies, waits for them, and re-layouts: 40.7 us -> 22.3 us
  matrix products: 24.4 us -> 40 us
  other arithmetic: 31.6 us -> 16.2 us
  between operations: 13.6 us -> 0.33 us
  starting transfers between devices: 5.91 us -> 16.2 us
    all_to_all x1 -> x0, waiting for transfers between devices: 200 us -> none  [local(): lax.all_to_all(produced, 'expert', split_axis=1, concat_axis=1, tiled=True)]
    all_to_all x3 -> x0, blocking collectives: 139 us -> none  [the longest x1 109 us: local(): lax.all_to_all(copy_rows, 'expert', split_axis=0, concat_axis=0, tiled=True)]
    ppermute x0 -> x22, waiting for transfers between devices: none -> 133 us  [the longest x4 43.9 us: local(): lax.ppermute(half[capacity:], 'expert', across)]
    reduce_sum x4 -> x1, other arithmetic: 24.1 us -> 0.11 us  [local(): weights = jnp.sum(jnp.where(pair_table, combine[:, :, None], 0.0), axis=1)]
    ppermute x0 -> x22, starting transfers between devices: none -> 16.2 us  [the longest x4 5.5 us: local(): other = lax.ppermute(own, 'expert', across)]
    gather x2 -> x0, local copies, waits for them, and re-layouts: 12.8 us -> none  [local(): picked = jnp.take(flat_gathered, slot_index, axis=0)]
    dot_general x1 -> x4, matrix products: 18.9 us -> 29.4 us  [expert_block(): jnp.dot(hidden, down_weight, preferred_element_type=jnp.float32)]
    another operation x1 -> x0, local copies, waits for them, and re-layouts: 7.97 us -> none  [local(): produced.reshape(replica_count, expert_rows, capacity, feature_width)]
  transfers between devices with their start and end apart: 2 -> 22, of which waited for: 2 -> 10; matrix products, arithmetic and copies ran while one was open for 0% -> 30% of each run, Pallas kernels for 0% -> 0%
where the time goes in v1:
time: 229 us; the launch traced here: 228 us
  waiting for transfers between devices  133 us (58%)
  matrix products  40 us (17%)
  local copies, waits for them, and re-layouts  22.3 us (10%)
  other arithmetic  16.2 us (7%)
  starting transfers between devices  16.2 us (7%)
    ppermute x4, waiting for transfers between devices, local(): lax.ppermute(half[capacity:], 'expert', across)  43.9 us
    ppermute x3, waiting for transfers between devices, local(): own = lax.ppermute(own, 'expert', shifted(step))  37.6 us
    dot_general x4, matrix products, expert_block(): jnp.dot(hidden, down_weight, preferred_element_type=jnp.float32)  29.4 us
    ppermute x3, waiting for transfers between devices, local(): whole = lax.ppermute(whole, 'expert', shifted(experts - step))  26.4 us
    ppermute x4, waiting for transfers between devices, local(): other = lax.ppermute(own, 'expert', across)  25 us
    dot_general x3, matrix products, expert_block(): gate_value = jnp.dot(rows, gate_weight, preferred_element_type=jnp.float32)  7.7 us
    unnamed x33, local copies, waits for them, and re-layouts  7.26 us
    slice x4, local copies, waits for them, and re-layouts, local(): produced[2 * capacity:]  6.6 us
  transfers between devices with their start and end apart: 22, of which 10 were waited for; matrix products, arithmetic and copies ran while one was open for 30% of the time, Pallas kernels for 0%

profile of v1, /device:TPU:0, one launch (start us, length us, event | category | flops | bytes accessed | tf_op | source)
XLA Modules:
  0.0 228.0 jit_solution(1674142708380150446)
XLA Ops:
  7.2 3.0 %collective-permute-start = (bf16[40,7168]{1,0:T(8,128)(2,1)S(1)}, bf16[40,7168]{1,0:T(8,128)(2,1)S(1)}, u32[]{:S(2)}, u32[]{:S(2)}) collective-permute-start(bf16[40,7168]{1,0:T(8,128)(2,1)S(1)} %get-tuple-element.5), channel_id=1, source_target_pairs={{0,2},{2,0},{4,6},{6,4},{8,10},{10,8},{12,14},{14,12},{1,3},{3,1},... | collective-permute-start | bytes 1720328 | tf_op jit(solution)/shard_map/ppermute | solution.py:71
  10.2 3.6 %collective-permute-start.16 = (bf16[40,7168]{1,0:T(8,128)(2,1)S(1)}, bf16[40,7168]{1,0:T(8,128)(2,1)}, u32[]{:S(2)}, u32[]{:S(2)}) collective-permute-start(bf16[40,7168]{1,0:T(8,128)(2,1)S(1)} %get-tuple-element.6), channel_id=1, source_target_pairs={{0,12},{2,14},{4,0},{6,2},{8,4},{10,6},{12,8},{14,10},{1,13},{3,15... | collective-permute-start | bytes 1720328 | tf_op jit(solution)/shard_map/ppermute | solution.py:70
  15.0 8.2 %collective-permute-done = bf16[40,7168]{1,0:T(8,128)(2,1)S(1)} collective-permute-done((bf16[40,7168]{1,0:T(8,128)(2,1)S(1)}, bf16[40,7168]{1,0:T(8,128)(2,1)S(1)}, u32[]{:S(2)}, u32[]{:S(2)}) %collective-permute-start) | collective-permute-done | bytes 573472 | tf_op jit(solution)/shard_map/ppermute | solution.py:71
  23.3 3.9 %collective-permute-done.16 = bf16[40,7168]{1,0:T(8,128)(2,1)} collective-permute-done((bf16[40,7168]{1,0:T(8,128)(2,1)S(1)}, bf16[40,7168]{1,0:T(8,128)(2,1)}, u32[]{:S(2)}, u32[]{:S(2)}) %collective-permute-start.16) | collective-permute-done | bytes 573472 | tf_op jit(solution)/shard_map/ppermute | solution.py:70
  28.9 33.7 %collective-permute-done.10 = bf16[40,7168]{1,0:T(8,128)(2,1)} collective-permute-done((bf16[40,7168]{1,0:T(8,128)(2,1)}, bf16[40,7168]{1,0:T(8,128)(2,1)}, u32[]{:S(2)}, u32[]{:S(2)}) %collective-permute-start.10) | collective-permute-done | bytes 573472 | tf_op jit(solution)/shard_map/ppermute | solution.py:70
  63.1 1.9 constant_dynamic-update-slice_fusion.5
  67.4 2.2 pad_maximum_fusion.4
  69.6 9.1 %collective-permute-done.11 = bf16[40,7168]{1,0:T(8,128)(2,1)S(1)} collective-permute-done((bf16[40,7168]{1,0:T(8,128)(2,1)}, bf16[40,7168]{1,0:T(8,128)(2,1)S(1)}, u32[]{:S(2)}, u32[]{:S(2)}) %collective-permute-start.11) | collective-permute-done | bytes 573472 | tf_op jit(solution)/shard_map/ppermute | solution.py:71
  78.8 2.2 pad_maximum_fusion.3
  81.0 7.7 %collective-permute-done.5 = bf16[40,7168]{1,0:T(8,128)(2,1)S(1)} collective-permute-done((bf16[40,7168]{1,0:T(8,128)(2,1)S(1)}, bf16[40,7168]{1,0:T(8,128)(2,1)S(1)}, u32[]{:S(2)}, u32[]{:S(2)}) %collective-permute-start.5) | collective-permute-done | bytes 573472 | tf_op jit(solution)/shard_map/ppermute | solution.py:71
  94.1 7.6 %convolution_convert_fusion.3 = bf16[160,7168]{1,0:T(8,128)(2,1)} fusion(bf16[256,7168]{1,0:T(8,128)(2,1)} %param.11, f32[160,256]{1,0:T(8,128)} %fusion.12, bf16[7168,256]{1,0:T(8,128)(2,1)} %param.9, bf16[80,7168]{1,0:T(8,128)(2,1)} %copy-done.12, bf16[40,7168]{1,0:T(8,128)(2,1)S(1)} %copy-done.10, bf16[40,7168]{1,0:T(8,128)(2,1)S(1)} %get-tuple-element.5), kind=kOutput, calls=%fused_computation.3 | convolution fusion | flops 1182679040 | bytes 12091392 | tf_op jit(solution)/shard_map/dot_general | solution.py:23
  106.5 7.2 %convolution_convert_fusion = bf16[160,7168]{1,0:T(8,128)(2,1)} fusion(bf16[256,7168]{1,0:T(8,128)(2,1)} %param.11, f32[160,256]{1,0:T(8,128)} %fusion.44, bf16[160,7168]{1,0:T(8,128)(2,1)S(1)} %constant_dynamic-update-slice_fusion.6, bf16[7168,256]{1,0:T(8,128)(2,1)} %param.10), kind=kOutput, calls=%fused_computation | convolution fusion | flops 1175797760 | bytes 12091392 | tf_op jit(solution)/shard_map/dot_general | solution.py:23
  113.8 2.5 %slice.105 = bf16[80,7168]{1,0:T(8,128)(2,1)} slice(bf16[160,7168]{1,0:T(8,128)(2,1)} %convolution_convert_fusion), slice={[80:160], [0:7168]} | slice | bytes 2293760 | tf_op jit(solution)/shard_map/slice | solution.py:78
  116.3 2.4 %constant_dynamic-update-slice_fusion.3 = bf16[160,7168]{1,0:T(8,128)(2,1)} fusion(bf16[160,7168]{1,0:T(8,128)(2,1)} %constant_dynamic-update-slice_fusion.4, bf16[80,7168]{1,0:T(8,128)(2,1)} %collective-permute-done.12), kind=kLoop, calls=%fused_computation.60 | loop fusion | bytes 2293760 | tf_op jit(solution)/shard_map/concatenate | solution.py:75
  118.6 3.1 %fusion.43 = f32[160,256]{1,0:T(8,128)} fusion(bf16[160,7168]{1,0:T(8,128)(2,1)} %constant_dynamic-update-slice_fusion.3, bf16[7168,256]{1,0:T(8,128)(2,1)S(1)} %copy-done.1), kind=kOutput, calls=%fused_computation.84 | convolution fusion | flops 587202560 | bytes 6127616 | tf_op jit(solution)/shard_map/dot_general | solution.py:20
  121.8 6.5 %convolution_convert_fusion.1 = bf16[160,7168]{1,0:T(8,128)(2,1)S(1)} fusion(bf16[256,7168]{1,0:T(8,128)(2,1)} %param.11, f32[160,256]{1,0:T(8,128)} %fusion.43, bf16[160,7168]{1,0:T(8,128)(2,1)} %constant_dynamic-update-slice_fusion.3, bf16[7168,256]{1,0:T(8,128)(2,1)} %param.10), kind=kOutput, calls=%fused_computation.1 | convolution fusion | flops 1175797760 | bytes 12091392 | tf_op jit(solution)/shard_map/dot_general | solution.py:23
  129.9 2.4 %constant_dynamic-update-slice_fusion = bf16[160,7168]{1,0:T(8,128)(2,1)} fusion(bf16[160,7168]{1,0:T(8,128)(2,1)} %constant_dynamic-update-slice_fusion.1, bf16[80,7168]{1,0:T(8,128)(2,1)} %collective-permute-done.6), kind=kLoop, calls=%fused_computation.57 | loop fusion | bytes 2293760 | tf_op jit(solution)/shard_map/concatenate | solution.py:75
  132.3 3.1 %fusion.42 = f32[160,256]{1,0:T(8,128)} fusion(bf16[160,7168]{1,0:T(8,128)(2,1)} %constant_dynamic-update-slice_fusion, bf16[7168,256]{1,0:T(8,128)(2,1)S(1)} %copy-done.2), kind=kOutput, calls=%fused_computation.83 | convolution fusion | flops 587202560 | bytes 6127616 | tf_op jit(solution)/shard_map/dot_general | solution.py:20
  135.4 8.1 %convolution_convert_fusion.2 = bf16[160,7168]{1,0:T(8,128)(2,1)} fusion(bf16[256,7168]{1,0:T(8,128)(2,1)} %param.11, f32[160,256]{1,0:T(8,128)} %fusion.42, bf16[160,7168]{1,0:T(8,128)(2,1)} %constant_dynamic-update-slice_fusion, bf16[7168,256]{1,0:T(8,128)(2,1)} %param.10), kind=kOutput, calls=%fused_computation.2 | convolution fusion | flops 1175797760 | bytes 12091392 | tf_op jit(solution)/shard_map/dot_general | solution.py:23
  155.2 20.3 %collective-permute-done.20 = bf16[40,7168]{1,0:T(8,128)(2,1)S(1)} collective-permute-done((bf16[40,7168]{1,0:T(8,128)(2,1)S(1)}, bf16[40,7168]{1,0:T(8,128)(2,1)S(1)}, u32[]{:S(2)}, u32[]{:S(2)}) %collective-permute-start.20) | collective-permute-done | bytes 573472 | tf_op jit(solution)/shard_map/ppermute | solution.py:80
  175.7 12.1 %collective-permute-done.14 = bf16[40,7168]{1,0:T(8,128)(2,1)S(1)} collective-permute-done((bf16[40,7168]{1,0:T(8,128)(2,1)S(1)}, bf16[40,7168]{1,0:T(8,128)(2,1)S(1)}, u32[]{:S(2)}, u32[]{:S(2)}) %collective-permute-start.14) | collective-permute-done | bytes 573472 | tf_op jit(solution)/shard_map/ppermute | solution.py:80
  188.0 11.5 %collective-permute-done.8 = bf16[40,7168]{1,0:T(8,128)(2,1)S(1)} collective-permute-done((bf16[40,7168]{1,0:T(8,128)(2,1)S(1)}, bf16[40,7168]{1,0:T(8,128)(2,1)S(1)}, u32[]{:S(2)}, u32[]{:S(2)}) %collective-permute-start.8) | collective-permute-done | bytes 573472 | tf_op jit(solution)/shard_map/ppermute | solution.py:80
  199.9 16.2 %collective-permute-done.15 = bf16[40,7168]{1,0:T(8,128)(2,1)S(1)} collective-permute-done((bf16[40,7168]{1,0:T(8,128)(2,1)S(1)}, bf16[40,7168]{1,0:T(8,128)(2,1)S(1)}, u32[]{:S(2)}, u32[]{:S(2)}) %collective-permute-start.15) | collective-permute-done | bytes 573472 | tf_op jit(solution)/shard_map/ppermute | solution.py:82
  216.0 10.2 %collective-permute-done.9 = bf16[40,7168]{1,0:T(8,128)(2,1)S(1)} collective-permute-done((bf16[40,7168]{1,0:T(8,128)(2,1)S(1)}, bf16[40,7168]{1,0:T(8,128)(2,1)S(1)}, u32[]{:S(2)}, u32[]{:S(2)}) %collective-permute-start.9) | collective-permute-done | bytes 573472 | tf_op jit(solution)/shard_map/ppermute | solution.py:82
  (106 shorter events, 38.9 us)
Async XLA Ops:
  7.2 15.9 %collective-permute-start = (bf16[40,7168]{1,0:T(8,128)(2,1)S(1)}, bf16[40,7168]{1,0:T(8,128)(2,1)S(1)}, u32[]{:S(2)}, u32[]{:S(2)}) collective-permute-start(bf16[40,7168]{1,0:T(8,128)(2,1)S(1)} %get-tuple-element.5), channel_id=1, source_target_pairs={{0,2},{2,0},{4,6},{6,4},{8,10},{10,8},{12,14},{14,12},{1,3},{3,1},... | collective-permute-start | bytes 1720328 | tf_op jit(solution)/shard_map/ppermute | solution.py:71
  10.2 17.1 %collective-permute-start.16 = (bf16[40,7168]{1,0:T(8,128)(2,1)S(1)}, bf16[40,7168]{1,0:T(8,128)(2,1)}, u32[]{:S(2)}, u32[]{:S(2)}) collective-permute-start(bf16[40,7168]{1,0:T(8,128)(2,1)S(1)} %get-tuple-element.6), channel_id=1, source_target_pairs={{0,12},{2,14},{4,0},{6,2},{8,4},{10,6},{12,8},{14,10},{1,13},{3,15... | collective-permute-start | bytes 1720328 | tf_op jit(solution)/shard_map/ppermute | solution.py:70
  13.8 48.8 %collective-permute-start.10 = (bf16[40,7168]{1,0:T(8,128)(2,1)}, bf16[40,7168]{1,0:T(8,128)(2,1)}, u32[]{:S(2)}, u32[]{:S(2)}) collective-permute-start(bf16[40,7168]{1,0:T(8,128)(2,1)} %get-tuple-element.7), channel_id=1, source_target_pairs={{0,8},{2,10},{4,12},{6,14},{8,0},{10,2},{12,4},{14,6},{1,9},{3,11}... | collective-permute-start | bytes 1720328 | tf_op jit(solution)/shard_map/ppermute | solution.py:70
  13.8 51.3 %collective-permute-start.4 = (bf16[40,7168]{1,0:T(8,128)(2,1)}, bf16[40,7168]{1,0:T(8,128)(2,1)S(1)}, u32[]{:S(2)}, u32[]{:S(2)}) collective-permute-start(bf16[40,7168]{1,0:T(8,128)(2,1)} %get-tuple-element.8), channel_id=1, source_target_pairs={{0,4},{2,6},{4,8},{6,10},{8,12},{10,14},{12,0},{14,2},{1,5},{3,7},... | collective-permute-start | bytes 1720328 | tf_op jit(solution)/shard_map/ppermute | solution.py:70
  23.3 68.3 %collective-permute-start.1 = (bf16[80,7168]{1,0:T(8,128)(2,1)S(1)}, bf16[80,7168]{1,0:T(8,128)(2,1)S(1)}, u32[]{:S(2)}, u32[]{:S(2)}) collective-permute-start(bf16[80,7168]{1,0:T(8,128)(2,1)S(1)} %pad_maximum_fusion.1), channel_id=1, source_target_pairs={{0,1},{1,0},{2,3},{3,2},{4,5},{5,4},{6,7},{7,6},{8,9},{9,8},{10,11... | collective-permute-start | bytes 3440648 | tf_op jit(solution)/shard_map/ppermute | solution.py:73
  27.3 40.2 %collective-permute-start.17 = (bf16[40,7168]{1,0:T(8,128)(2,1)}, bf16[40,7168]{1,0:T(8,128)(2,1)S(1)}, u32[]{:S(2)}, u32[]{:S(2)}) collective-permute-start(bf16[40,7168]{1,0:T(8,128)(2,1)} %collective-permute-done.16), channel_id=1, source_target_pairs={{0,2},{2,0},{4,6},{6,4},{8,10},{10,8},{12,14},{14,12},{1,3},{3,1},... | collective-permute-start | bytes 1720328 | tf_op jit(solution)/shard_map/ppermute | solution.py:71
  62.6 16.1 %collective-permute-start.11 = (bf16[40,7168]{1,0:T(8,128)(2,1)}, bf16[40,7168]{1,0:T(8,128)(2,1)S(1)}, u32[]{:S(2)}, u32[]{:S(2)}) collective-permute-start(bf16[40,7168]{1,0:T(8,128)(2,1)} %collective-permute-done.10), channel_id=1, source_target_pairs={{0,2},{2,0},{4,6},{6,4},{8,10},{10,8},{12,14},{14,12},{1,3},{3,1},... | collective-permute-start | bytes 1720328 | tf_op jit(solution)/shard_map/ppermute | solution.py:71
  65.1 23.6 %collective-permute-start.5 = (bf16[40,7168]{1,0:T(8,128)(2,1)S(1)}, bf16[40,7168]{1,0:T(8,128)(2,1)S(1)}, u32[]{:S(2)}, u32[]{:S(2)}) collective-permute-start(bf16[40,7168]{1,0:T(8,128)(2,1)S(1)} %collective-permute-done.4), channel_id=1, source_target_pairs={{0,2},{2,0},{4,6},{6,4},{8,10},{10,8},{12,14},{14,12},{1,3},{3,1},... | collective-permute-start | bytes 1720328 | tf_op jit(solution)/shard_map/ppermute | solution.py:71
  69.6 34.1 %collective-permute-start.18 = (bf16[80,7168]{1,0:T(8,128)(2,1)}, bf16[80,7168]{1,0:T(8,128)(2,1)}, u32[]{:S(2)}, u32[]{:S(2)}) collective-permute-start(bf16[80,7168]{1,0:T(8,128)(2,1)} %pad_maximum_fusion.4), channel_id=1, source_target_pairs={{0,1},{1,0},{2,3},{3,2},{4,5},{5,4},{6,7},{7,6},{8,9},{9,8},{10,11... | collective-permute-start | bytes 3440648 | tf_op jit(solution)/shard_map/ppermute | solution.py:73
  81.0 11.6 %copy-start.3 = (bf16[7168,256]{1,0:T(8,128)(2,1)S(1)}, bf16[7168,256]{1,0:T(8,128)(2,1)}, u32[]{:S(2)}) copy-start(bf16[7168,256]{1,0:T(8,128)(2,1)} %param.10) | copy-start | bytes 11010052
  81.0 11.6 %copy-start.9 = (bf16[40,7168]{1,0:T(8,128)(2,1)S(1)}, bf16[40,7168]{1,0:T(8,128)(2,1)}, u32[]{:S(2)}) copy-start(bf16[40,7168]{1,0:T(8,128)(2,1)} %copy-done.8) | copy-start | bytes 1720324
  81.0 35.3 %collective-permute-start.12 = (bf16[80,7168]{1,0:T(8,128)(2,1)}, bf16[80,7168]{1,0:T(8,128)(2,1)}, u32[]{:S(2)}, u32[]{:S(2)}) collective-permute-start(bf16[80,7168]{1,0:T(8,128)(2,1)} %pad_maximum_fusion.3), channel_id=1, source_target_pairs={{0,1},{1,0},{2,3},{3,2},{4,5},{5,4},{6,7},{7,6},{8,9},{9,8},{10,11... | collective-permute-start | bytes 3440648 | tf_op jit(solution)/shard_map/ppermute | solution.py:73
  89.8 40.1 %collective-permute-start.6 = (bf16[80,7168]{1,0:T(8,128)(2,1)}, bf16[80,7168]{1,0:T(8,128)(2,1)}, u32[]{:S(2)}, u32[]{:S(2)}) collective-permute-start(bf16[80,7168]{1,0:T(8,128)(2,1)} %pad_maximum_fusion.2), channel_id=1, source_target_pairs={{0,1},{1,0},{2,3},{3,2},{4,5},{5,4},{6,7},{7,6},{8,9},{9,8},{10,11... | collective-permute-start | bytes 3440648 | tf_op jit(solution)/shard_map/ppermute | solution.py:73
  103.1 42.3 %collective-permute-start.2 = (bf16[80,7168]{1,0:T(8,128)(2,1)S(1)}, bf16[80,7168]{1,0:T(8,128)(2,1)}, u32[]{:S(2)}, u32[]{:S(2)}) collective-permute-start(bf16[80,7168]{1,0:T(8,128)(2,1)S(1)} %slice.90), channel_id=1, source_target_pairs={{0,1},{1,0},{2,3},{3,2},{4,5},{5,4},{6,7},{7,6},{8,9},{9,8},{10,11... | collective-permute-start | bytes 3440648 | tf_op jit(solution)/shard_map/ppermute | solution.py:78
  116.2 31.7 %collective-permute-start.19 = (bf16[80,7168]{1,0:T(8,128)(2,1)}, bf16[80,7168]{1,0:T(8,128)(2,1)}, u32[]{:S(2)}, u32[]{:S(2)}) collective-permute-start(bf16[80,7168]{1,0:T(8,128)(2,1)} %slice.105), channel_id=1, source_target_pairs={{0,1},{1,0},{2,3},{3,2},{4,5},{5,4},{6,7},{7,6},{8,9},{9,8},{10,11... | collective-permute-start | bytes 3440648 | tf_op jit(solution)/shard_map/ppermute | solution.py:78
  129.4 21.7 %collective-permute-start.13 = (bf16[80,7168]{1,0:T(8,128)(2,1)}, bf16[80,7168]{1,0:T(8,128)(2,1)}, u32[]{:S(2)}, u32[]{:S(2)}) collective-permute-start(bf16[80,7168]{1,0:T(8,128)(2,1)} %slice.100), channel_id=1, source_target_pairs={{0,1},{1,0},{2,3},{3,2},{4,5},{5,4},{6,7},{7,6},{8,9},{9,8},{10,11... | collective-permute-start | bytes 3440648 | tf_op jit(solution)/shard_map/ppermute | solution.py:78
  145.1 8.3 %collective-permute-start.7 = (bf16[80,7168]{1,0:T(8,128)(2,1)S(1)}, bf16[80,7168]{1,0:T(8,128)(2,1)S(1)}, u32[]{:S(2)}, u32[]{:S(2)}) collective-permute-start(bf16[80,7168]{1,0:T(8,128)(2,1)S(1)} %slice.95), channel_id=1, source_target_pairs={{0,1},{1,0},{2,3},{3,2},{4,5},{5,4},{6,7},{7,6},{8,9},{9,8},{10,11... | collective-permute-start | bytes 3440648 | tf_op jit(solution)/shard_map/ppermute | solution.py:78
  147.3 52.4 %collective-permute-start.3 = (bf16[40,7168]{1,0:T(8,128)(2,1)S(1)}, bf16[40,7168]{1,0:T(8,128)(2,1)S(1)}, u32[]{:S(2)}, u32[]{:S(2)}) collective-permute-start(bf16[40,7168]{1,0:T(8,128)(2,1)S(1)} %slice.92), channel_id=1, source_target_pairs={{0,2},{2,0},{4,6},{6,4},{8,10},{10,8},{12,14},{14,12},{1,3},{3,1},... | collective-permute-start | bytes 1720328 | tf_op jit(solution)/shard_map/ppermute | solution.py:80
  149.5 26.0 %collective-permute-start.20 = (bf16[40,7168]{1,0:T(8,128)(2,1)S(1)}, bf16[40,7168]{1,0:T(8,128)(2,1)S(1)}, u32[]{:S(2)}, u32[]{:S(2)}) collective-permute-start(bf16[40,7168]{1,0:T(8,128)(2,1)S(1)} %slice.107), channel_id=1, source_target_pairs={{0,2},{2,0},{4,6},{6,4},{8,10},{10,8},{12,14},{14,12},{1,3},{3,1},... | collective-permute-start | bytes 1720328 | tf_op jit(solution)/shard_map/ppermute | solution.py:80
  152.7 35.1 %collective-permute-start.14 = (bf16[40,7168]{1,0:T(8,128)(2,1)S(1)}, bf16[40,7168]{1,0:T(8,128)(2,1)S(1)}, u32[]{:S(2)}, u32[]{:S(2)}) collective-permute-start(bf16[40,7168]{1,0:T(8,128)(2,1)S(1)} %slice.102), channel_id=1, source_target_pairs={{0,2},{2,0},{4,6},{6,4},{8,10},{10,8},{12,14},{14,12},{1,3},{3,1},... | collective-permute-start | bytes 1720328 | tf_op jit(solution)/shard_map/ppermute | solution.py:80
  153.7 45.8 %collective-permute-start.8 = (bf16[40,7168]{1,0:T(8,128)(2,1)S(1)}, bf16[40,7168]{1,0:T(8,128)(2,1)S(1)}, u32[]{:S(2)}, u32[]{:S(2)}) collective-permute-start(bf16[40,7168]{1,0:T(8,128)(2,1)S(1)} %slice.97), channel_id=1, source_target_pairs={{0,2},{2,0},{4,6},{6,4},{8,10},{10,8},{12,14},{14,12},{1,3},{3,1},... | collective-permute-start | bytes 1720328 | tf_op jit(solution)/shard_map/ppermute | solution.py:80
  175.6 24.2 %collective-permute-start.21 = (bf16[40,7168]{1,0:T(8,128)(2,1)S(1)}, bf16[40,7168]{1,0:T(8,128)(2,1)S(1)}, u32[]{:S(2)}, u32[]{:S(2)}) collective-permute-start(bf16[40,7168]{1,0:T(8,128)(2,1)S(1)} %add_convert_fusion.4), channel_id=1, source_target_pairs={{0,4},{2,6},{4,8},{6,10},{8,12},{10,14},{12,0},{14,2},{1,5},{3,7},... | collective-permute-start | bytes 1720328 | tf_op jit(solution)/shard_map/ppermute | solution.py:82
  187.9 28.1 %collective-permute-start.15 = (bf16[40,7168]{1,0:T(8,128)(2,1)S(1)}, bf16[40,7168]{1,0:T(8,128)(2,1)S(1)}, u32[]{:S(2)}, u32[]{:S(2)}) collective-permute-start(bf16[40,7168]{1,0:T(8,128)(2,1)S(1)} %add_convert_fusion.5), channel_id=1, source_target_pairs={{0,8},{2,10},{4,12},{6,14},{8,0},{10,2},{12,4},{14,6},{1,9},{3,11}... | collective-permute-start | bytes 1720328 | tf_op jit(solution)/shard_map/ppermute | solution.py:82
  199.6 26.6 %collective-permute-start.9 = (bf16[40,7168]{1,0:T(8,128)(2,1)S(1)}, bf16[40,7168]{1,0:T(8,128)(2,1)S(1)}, u32[]{:S(2)}, u32[]{:S(2)}) collective-permute-start(bf16[40,7168]{1,0:T(8,128)(2,1)S(1)} %add_convert_fusion.6), channel_id=1, source_target_pairs={{0,12},{2,14},{4,0},{6,2},{8,4},{10,6},{12,8},{14,10},{1,13},{3,15... | collective-permute-start | bytes 1720328 | tf_op jit(solution)/shard_map/ppermute | solution.py:82
  (11 other events, 38.7 us)

commit v2 on v1

v2 whole, which is shorter than its diff:
```python
import functools

import jax
import jax.numpy as jnp
from jax import lax
from jax.experimental import pallas as pl
from jax.experimental.pallas import tpu as pltpu
from jax.sharding import PartitionSpec as P

SLICES = 4
SPLIT = True
FIRST = (1, -1)
GATES = {
    "a0": ("b3",),
    "a2": ("o3",),
    "a3": ("b2", "h1",),
    "c2": ("b1",),
    "y3": ("b1",),
    "z2": ("w1",),
    "z3": ("o0", "w2",),
}


FREE = pl.CostEstimate(flops=0, bytes_accessed=0, transcendentals=0)


def pack_kernel(order, home_ref, ids_ref, tokens_ref, *refs):
    piece_refs, rows_ref = refs[:-1], refs[-1]
    experts = len(order)
    capacity = piece_refs[0].shape[0]
    row_count, width = tokens_ref.shape
    for begin in range(0, width, 128):
        block = tokens_ref[:, begin : begin + 128].astype(jnp.float32)
        scale = jnp.max(jnp.abs(block), axis=1, keepdims=True) / 448.0 + 1e-06
        scale = scale.astype(jnp.bfloat16).astype(jnp.float32)
        quantized = (block / scale).astype(jnp.bfloat16).astype(jnp.float32)
        rows_ref[:, begin : begin + 128] = (quantized * scale).astype(jnp.bfloat16)
    distance = ids_ref[...] - home_ref[0]
    distance = jnp.where(distance < 0, distance + experts, distance)
    chunk_of = lax.broadcasted_iota(jnp.int32, (experts, row_count), 0)
    step_of = jnp.zeros_like(chunk_of)
    for k, step in enumerate(order):
        step_of = jnp.where(chunk_of == k, step, step_of)
    member = jnp.zeros((experts, row_count), jnp.float32)
    for route in range(ids_ref.shape[0]):
        member = member + (step_of == distance[route : route + 1]).astype(jnp.float32)
    before = lax.broadcasted_iota(jnp.int32, (row_count, row_count), 0)
    before = before < lax.broadcasted_iota(jnp.int32, (row_count, row_count), 1)
    position = jnp.dot(
        member.astype(jnp.bfloat16),
        before.astype(jnp.float32).astype(jnp.bfloat16),
        preferred_element_type=jnp.float32,
    )
    slot = lax.broadcasted_iota(jnp.int32, (capacity, row_count), 0).astype(jnp.float32)
    columns = width // 4
    for k in range(experts):
        place = jnp.where(slot == position[k : k + 1], member[k : k + 1], 0.0).astype(jnp.bfloat16)
        for begin in range(0, width, columns):
            part = slice(begin, begin + columns)
            picked = jnp.dot(place, rows_ref[:, part], preferred_element_type=jnp.float32)
            piece_refs[k][:, part] = picked.astype(jnp.bfloat16)


def packed(tokens, expert_ids, home, order, capacity):
    shape = jax.ShapeDtypeStruct((capacity, tokens.shape[1]), jnp.bfloat16)
    vmem = pl.BlockSpec(memory_space=pltpu.VMEM)
    return pl.pallas_call(
        functools.partial(pack_kernel, order),
        in_specs=[pl.BlockSpec(memory_space=pltpu.SMEM), vmem, vmem],
        out_specs=[vmem] * len(order),
        out_shape=[shape] * len(order),
        scratch_shapes=[pltpu.VMEM(tokens.shape, jnp.bfloat16)],
        compiler_params=pltpu.CompilerParams(vmem_limit_bytes=24 << 20),
    )(home.reshape(1), expert_ids.T, tokens)


def hidden_kernel(steps, rows_ref, gate_ref, up_ref, hidden_ref, gate_sum, up_sum):
    step = pl.program_id(0)
    rows = rows_ref[...]
    gate = jnp.dot(rows, gate_ref[...], preferred_element_type=jnp.float32)
    up = jnp.dot(rows, up_ref[...], preferred_element_type=jnp.float32)

    @pl.when(step == 0)
    def _():
        gate_sum[...] = gate
        up_sum[...] = up

    @pl.when(step > 0)
    def _():
        gate_sum[...] += gate
        up_sum[...] += up

    @pl.when(step == steps - 1)
    def _():
        value = gate_sum[...]
        hidden_ref[...] = (value / (1.0 + jnp.exp(-value)) * up_sum[...]).astype(jnp.bfloat16)


def hidden_of(rows, gate_weight, up_weight, steps=4):
    count, width = rows.shape
    units = gate_weight.shape[1]
    depth = width // steps
    return pl.pallas_call(
        functools.partial(hidden_kernel, steps),
        grid=(steps,),
        in_specs=[
            pl.BlockSpec((count, depth), lambda i: (0, i)),
            pl.BlockSpec((depth, units), lambda i: (i, 0)),
            pl.BlockSpec((depth, units), lambda i: (i, 0)),
        ],
        out_specs=pl.BlockSpec((count, units), lambda i: (0, 0)),
        out_shape=jax.ShapeDtypeStruct((count, units), jnp.bfloat16),
        scratch_shapes=[pltpu.VMEM((count, units), jnp.float32)] * 2,
        compiler_params=pltpu.CompilerParams(vmem_limit_bytes=16 << 20),
        cost_estimate=FREE,
    )(rows, gate_weight, up_weight)


def down_kernel(hidden_ref, down_ref, near_ref, away_ref):
    made = jnp.dot(hidden_ref[...], down_ref[...], preferred_element_type=jnp.float32)
    half = near_ref.shape[0]
    near_ref[...] = made[:half].astype(jnp.bfloat16)
    away_ref[...] = made[half:].astype(jnp.bfloat16)


def outputs_of(hidden, down_weight, steps=2):
    count, units = hidden.shape
    width = down_weight.shape[1]
    columns = width // steps
    return pl.pallas_call(
        down_kernel,
        grid=(steps,),
        in_specs=[
            pl.BlockSpec((count, units), lambda i: (0, 0)),
            pl.BlockSpec((units, columns), lambda i: (0, i)),
        ],
        out_specs=[pl.BlockSpec((count // 2, columns), lambda i: (0, i))] * 2,
        out_shape=[jax.ShapeDtypeStruct((count // 2, width), jnp.bfloat16)] * 2,
        compiler_params=pltpu.CompilerParams(vmem_limit_bytes=16 << 20),
        cost_estimate=FREE,
    )(hidden, down_weight)


def no_rows(width, *earlier):
    zero = jnp.zeros((1, width), jnp.float32)
    for rows in earlier:
        row = rows[:1].astype(jnp.float32) * 0.0
        if row.shape[1] < width:
            row = jnp.concatenate([row] * (width // row.shape[1]), axis=1)
        zero = zero + row[:, :width]
    return zero


def hold(rows, *earlier):
    return (rows.astype(jnp.float32) + no_rows(rows.shape[1], *earlier)).astype(jnp.bfloat16)


def add_rows(left, right):
    return (left.astype(jnp.float32) + right.astype(jnp.float32)).astype(jnp.bfloat16)


def local(tokens, expert_ids, router_values, gate_weight, up_weight, down_weight):
    row_count, width = tokens.shape
    route_count = expert_ids.shape[1]
    replicas = lax.axis_size("dp")
    chips = lax.axis_size("expert")
    experts = chips * replicas // SLICES
    per = chips // experts
    capacity = row_count * route_count // experts * 5 // 4
    assert replicas == 2 and per == 2 and experts >= 4
    wide = width // 2

    home = lax.axis_index("expert") // per
    core = lax.axis_index("dp")
    across = [(i, i ^ 1) for i in range(chips)]

    def along(rows, step):
        return lax.ppermute(
            rows, "expert", [(i, (i + per * step) % chips) for i in range(chips)]
        )

    def over(rows):
        return lax.ppermute(rows, "expert", across)

    def swap(rows):
        return lax.ppermute(rows, "dp", [(0, 1), (1, 0)])

    order = [0] + [step % experts for step in FIRST]
    order += [step for step in range(experts) if step not in order]
    last = experts - 1

    combine = 2.5 * router_values / jnp.sum(router_values, axis=1, keepdims=True)
    distance = lax.rem(expert_ids - home + experts, experts)
    chosen = jnp.zeros_like(distance)
    for k, step in enumerate(order):
        chosen = jnp.where(distance == step, k, chosen)
    chosen = chosen.reshape(row_count * route_count)
    member = (chosen[:, None] == jnp.arange(experts, dtype=jnp.int32)[None, :]).astype(jnp.int32)
    earlier_rows = jnp.cumsum(member, axis=0) - member
    position = jnp.sum(earlier_rows * member, axis=1)
    slot_index = (chosen * (2 * capacity) + position).reshape(row_count, route_count)
    slots = jnp.arange(experts * 2 * capacity, dtype=jnp.int32)
    pair_table = slot_index[:, :, None] == slots[None, None, :]
    weights = jnp.sum(jnp.where(pair_table, combine[:, :, None], 0.0), axis=1)
    weights_high = lax.reduce_precision(weights, 8, 7)
    weights_low = weights - weights_high
    my_weights = jnp.concatenate([weights_high, weights_low], axis=0).astype(jnp.bfloat16)
    peer_weights = swap(my_weights)
    peer_weights = jnp.concatenate(
        [jnp.zeros((2 * row_count, capacity), jnp.bfloat16), peer_weights[:, :-capacity]], axis=1
    )
    all_weights = jnp.concatenate([my_weights, peer_weights], axis=0)

    down_far = swap(lax.dynamic_slice_in_dim(down_weight, (1 - core) * wide, wide, 1))
    down_near = lax.dynamic_slice_in_dim(down_weight, core * wide, wide, 1)
    down_half = jnp.concatenate([down_near, down_far], axis=0)

    pieces = packed(tokens, expert_ids, home, tuple(order), capacity)

    def piece(k, low, high, *earlier):
        part = pieces[k] if high - low == capacity else pieces[k][low:high]
        return hold(part, *earlier) if earlier else part

    seen = {}

    def gates(point):
        return [seen[name] for name in GATES.get(point, ()) if name in seen]

    def maybe_hold(rows, point):
        found = gates(point)
        return hold(rows, *found) if found else rows

    own, own_far, near, raw = {}, {}, {}, {}

    def dispatch(k):
        if k == 0:
            own[k] = piece(k, 0, capacity)
        elif order[k] == 2 and SPLIT:
            half = (capacity // 2 + 7) // 8 * 8
            upper = along(piece(k, 0, half, *gates("z%d" % k)), order[k])
            seen["u3"] = upper
            lower = along(piece(k, half, capacity, upper, *gates("z%db" % k)), order[k])
            own[k] = jnp.concatenate([upper, lower], axis=0)
        else:
            own[k] = along(piece(k, 0, capacity, *gates("z%d" % k)), order[k])
        seen["w%d" % k] = own[k]

    def spread(k):
        own[k] = maybe_hold(own[k], "y%d" % k)
        own_far[k] = swap(own[k])
        seen["o%d" % k] = over(own[k])

    def turned(hidden):
        quarters = [hidden[i * capacity : (i + 1) * capacity] for i in range(4)]
        return jnp.concatenate([quarters[i] for i in (1, 0, 3, 2)], axis=0)

    def compute(k):
        other = maybe_hold(seen["o%d" % k], "c%d" % k)
        flat = jnp.concatenate([own[k], own_far[k], other, swap(other)], axis=0)
        hidden = hidden_of(flat, gate_weight, up_weight)
        hidden = jnp.concatenate([hidden, turned(swap(hidden))], axis=1)
        near[k], raw[k] = outputs_of(hidden, down_half)
        seen["n%d" % k] = near[k]

    def merge(k):
        seen["b%d" % k] = over(maybe_hold(raw[k], "a%d" % k))

    def give_back(k):
        total = add_rows(near[k], seen["b%d" % k])
        seen["h%d" % k] = along(total, -order[k]) if k else total

    for k in range(3):
        dispatch(k)
        spread(k)
    dispatch(3)
    compute(1)
    for k in range(2, last):
        merge(k - 1)
        compute(k)
        spread(k + 1)
        give_back(k - 1)
        if k + 2 < experts:
            dispatch(k + 2)
    compute(0)
    merge(last - 1)
    compute(last)
    merge(last)
    give_back(last - 1)
    merge(0)
    give_back(last)
    give_back(0)
    whole = [seen["h%d" % k] for k in range(experts)]
    returned = jnp.concatenate(whole, axis=0)
    product = jnp.dot(all_weights, returned, preferred_element_type=jnp.float32)
    product = product.reshape(2, 2, row_count, wide)
    halves = (product[:, 0] + product[:, 1]).astype(jnp.bfloat16)
    mine, got = halves[0], swap(halves[1])
    return jnp.where(
        core == 0,
        jnp.concatenate([mine, got], axis=1),
        jnp.concatenate([got, mine], axis=1),
    )


def solution(mesh):
    in_specs = (
        P(("groups", "expert", "dp"), None),
        P(("groups", "expert", "dp"), None),
        P(("groups", "expert", "dp"), None),
        P(None, ("expert", "dp")),
        P(None, ("expert", "dp")),
        P(("expert", "dp"), None),
    )
    out_specs = P(("groups", "expert", "dp"), None)
    return jax.shard_map(local, mesh=mesh, in_specs=in_specs, out_specs=out_specs, check_vma=False)
```

time: 229 us -> 157 us (0.69)
  matrix products: 40 us -> 2.01 us
  waiting for transfers between devices: 133 us -> 109 us
  local copies, waits for them, and re-layouts: 22.3 us -> 4.86 us
  Pallas kernels: 0 us -> 15.8 us
  other arithmetic: 16.2 us -> 9.53 us
    dot_general x10 -> x1, matrix products: 40 us -> 2.01 us  [local(): product = jnp.dot(all_weights, returned, preferred_element_type=jnp.float32)]
    ppermute x22 -> x30, waiting for transfers between devices: 133 us -> 109 us  [the longest x8 60.4 us: over(): return lax.ppermute(rows, 'expert', across)]
    pallas_call x0 -> x9, Pallas kernels: none -> 15.8 us  [the longest x4 9.1 us: hidden_of(): pl.pallas_call(functools.partial(hidden_kernel, steps), grid=(steps,), in...]
    slice x9 -> x5, local copies, waits for them, and re-layouts: 7.92 us -> 0.05 us  [the longest x4 0.03 us: turned(): quarters = [hidden[i * capacity:(i + 1) * capacity] for i in range(4)]]
    concatenate x3 -> x0, local copies, waits for them, and re-layouts: 6.14 us -> none  [local(): jnp.concatenate([pair, far], axis=0)]
    unnamed x33 -> x8, local copies, waits for them, and re-layouts: 7.26 us -> 1.87 us
    convert_element_type x8 -> x4, other arithmetic: 5.6 us -> 0.55 us  [add_rows(): (left.astype(jnp.float32) + right.astype(jnp.float32)).astype(jnp.bfloat16)]
    concatenate x4 -> x11, other arithmetic: 5.55 us -> 2.64 us  [the longest x4 1.67 us: compute(): flat = jnp.concatenate([own[k], own_far[k], other, swap(other)], axis=0)]
  transfers between devices with their start and end apart: 22 -> 30, of which waited for: 10 -> 14; matrix products, arithmetic and copies ran while one was open for 30% -> 7% of each run, Pallas kernels for 0% -> 9%
where the time goes in v2:
time: 157 us; the launch traced here: 156 us
  waiting for transfers between devices  109 us (69%)
  Pallas kernels  15.8 us (10%)
  starting transfers between devices  14.1 us (9%)
  other arithmetic  9.53 us (6%)
  local copies, waits for them, and re-layouts  4.86 us (3%)
  matrix products  2.01 us (1%)
    ppermute x8, waiting for transfers between devices, over(): return lax.ppermute(rows, 'expert', across)  60.4 us
    ppermute x7, waiting for transfers between devices, along(): lax.ppermute(rows, 'expert', [(i, (i + per * step) % chips) for i in rang...  44.1 us
    pallas_call x4, Pallas kernels, hidden_of(): pl.pallas_call(functools.partial(hidden_kernel, steps), grid=(steps,), in...  9.1 us
    ppermute x8, starting transfers between devices, over(): return lax.ppermute(rows, 'expert', across)  6.97 us
    ppermute x7, starting transfers between devices, along(): lax.ppermute(rows, 'expert', [(i, (i + per * step) % chips) for i in rang...  5.23 us
    pallas_call x4, Pallas kernels, outputs_of(): pl.pallas_call(down_kernel, grid=(steps,), in_specs=[pl.BlockSpec((count,...  5.16 us
    ppermute x15, waiting for transfers between devices, swap(): return lax.ppermute(rows, 'dp', [(0, 1), (1, 0)])  4.84 us
  transfers between devices with their start and end apart: 30, of which 14 were waited for; matrix products, arithmetic and copies ran while one was open for 7% of the time, Pallas kernels for 9%

profile of v2, /device:TPU:0, one launch (start us, length us, event | category | flops | bytes accessed | tf_op | source)
XLA Modules:
  0.0 156.2 jit_solution(4532199570469852572)
XLA Ops:
  1.9 1.6 shard_map.64
  3.4 3.0 %collective-permute-start.2 = (bf16[40,7168]{1,0:T(8,128)(2,1)S(1)}, bf16[40,7168]{1,0:T(8,128)(2,1)S(1)}, u32[]{:S(2)}, u32[]{:S(2)}) collective-permute-start(bf16[40,7168]{1,0:T(8,128)(2,1)S(1)} %get-tuple-element.17), channel_id=1, source_target_pairs={{0,2},{2,0},{4,6},{6,4},{8,10},{10,8},{12,14},{14,12},{1,3},{3,1},... | collective-permute-start | bytes 1720328 | tf_op jit(solution)/shard_map/ppermute | solution.py:183
  6.5 1.6 %collective-permute-start.6 = (bf16[40,7168]{1,0:T(8,128)(2,1)S(1)}, bf16[40,7168]{1,0:T(8,128)(2,1)S(1)}, u32[]{:S(2)}, u32[]{:S(2)}) collective-permute-start(bf16[40,7168]{1,0:T(8,128)(2,1)S(1)} %get-tuple-element.22), channel_id=1, source_target_pairs={{0,4},{2,6},{4,8},{6,10},{8,12},{10,14},{12,0},{14,2},{1,5},{3,7},... | collective-permute-start | bytes 1720328 | tf_op jit(solution)/shard_map/ppermute | solution.py:178
  13.5 2.4 %constant_dynamic-slice_fusion = (bf16[256,3584]{1,0:T(8,128)(2,1)S(1)}, bf16[256,3584]{1,0:T(8,128)(2,1)S(1)}) fusion(bf16[256,7168]{1,0:T(8,128)(2,1)} %param.11, s32[]{:T(128)S(6)} %select_n.40, s32[]{:T(128)S(6)} %select_n.41), kind=kLoop, calls=%fused_computation.82 | loop fusion | bytes 7340040 | tf_op jit(solution)/shard_map/dynamic_slice | solution.py:215
  16.3 7.4 %collective-permute-done.6 = bf16[40,7168]{1,0:T(8,128)(2,1)S(1)} collective-permute-done((bf16[40,7168]{1,0:T(8,128)(2,1)S(1)}, bf16[40,7168]{1,0:T(8,128)(2,1)S(1)}, u32[]{:S(2)}, u32[]{:S(2)}) %collective-permute-start.6) | collective-permute-done | bytes 573472 | tf_op jit(solution)/shard_map/ppermute | solution.py:178
  23.9 1.8 %collective-permute-start.7 = (bf16[40,7168]{1,0:T(8,128)(2,1)S(1)}, bf16[40,7168]{1,0:T(8,128)(2,1)S(1)}, u32[]{:S(2)}, u32[]{:S(2)}) collective-permute-start(bf16[40,7168]{1,0:T(8,128)(2,1)S(1)} %add_convert_fusion.9), channel_id=1, source_target_pairs={{0,12},{2,14},{4,0},{6,2},{8,4},{10,6},{12,8},{14,10},{1,13},{3,15... | collective-permute-start | bytes 1720328 | tf_op jit(solution)/shard_map/ppermute | solution.py:178
  27.5 2.3 %shard_map.65 = bf16[160,256]{1,0:T(8,128)(2,1)S(1)} custom-call(bf16[160,7168]{1,0:T(8,128)(2,1)S(1)} %pad_maximum_fusion.1.rows_ref, bf16[7168,256]{1,0:T(8,128)(2,1)S(1)} %copy-done, bf16[7168,256]{1,0:T(8,128)(2,1)S(1)} %copy-done.1), custom_call_target="tpu_custom_call" | custom-call | tf_op jit(solution)/shard_map/pallas_call | solution.py:103
  29.8 9.6 %collective-permute-done.7 = bf16[40,7168]{1,0:T(8,128)(2,1)S(1)} collective-permute-done((bf16[40,7168]{1,0:T(8,128)(2,1)S(1)}, bf16[40,7168]{1,0:T(8,128)(2,1)S(1)}, u32[]{:S(2)}, u32[]{:S(2)}) %collective-permute-start.7) | collective-permute-done | bytes 573472 | tf_op jit(solution)/shard_map/ppermute | solution.py:178
  39.4 1.5 collective-permute-done.11
  43.1 2.3 %shard_map.67 = bf16[160,256]{1,0:T(8,128)(2,1)S(1)} custom-call(bf16[160,7168]{1,0:T(8,128)(2,1)S(1)} %pad_maximum_fusion.2.rows_ref, bf16[7168,256]{1,0:T(8,128)(2,1)S(1)} %copy-done, bf16[7168,256]{1,0:T(8,128)(2,1)S(1)} %copy-done.1), custom_call_target="tpu_custom_call" | custom-call | tf_op jit(solution)/shard_map/pallas_call | solution.py:103
  45.4 14.4 %collective-permute-done.8 = bf16[24,7168]{1,0:T(8,128)(2,1)S(1)} collective-permute-done((bf16[24,7168]{1,0:T(8,128)(2,1)S(1)}, bf16[24,7168]{1,0:T(8,128)(2,1)S(1)}, u32[]{:S(2)}, u32[]{:S(2)}) %collective-permute-start.8) | collective-permute-done | bytes 344096 | tf_op jit(solution)/shard_map/ppermute | solution.py:178
  63.3 14.4 %collective-permute-done.14 = bf16[80,3584]{1,0:T(8,128)(2,1)S(1)} collective-permute-done((bf16[80,3584]{1,0:T(8,128)(2,1)S(1)}, bf16[80,3584]{1,0:T(8,128)(2,1)S(1)}, u32[]{:S(2)}, u32[]{:S(2)}) %collective-permute-start.14) | collective-permute-done | bytes 573472 | tf_op jit(solution)/shard_map/ppermute | solution.py:183
  81.5 2.3 %shard_map.71 = bf16[160,256]{1,0:T(8,128)(2,1)S(1)} custom-call(bf16[160,7168]{1,0:T(8,128)(2,1)S(1)} %pad_maximum_fusion.4.rows_ref, bf16[7168,256]{1,0:T(8,128)(2,1)S(1)} %copy-done, bf16[7168,256]{1,0:T(8,128)(2,1)S(1)} %copy-done.1), custom_call_target="tpu_custom_call" | custom-call | tf_op jit(solution)/shard_map/pallas_call | solution.py:103
  84.0 8.3 %collective-permute-done.16 = bf16[40,7168]{1,0:T(8,128)(2,1)S(1)} collective-permute-done((bf16[40,7168]{1,0:T(8,128)(2,1)S(1)}, bf16[40,7168]{1,0:T(8,128)(2,1)S(1)}, u32[]{:S(2)}, u32[]{:S(2)}) %collective-permute-start.16) | collective-permute-done | bytes 573472 | tf_op jit(solution)/shard_map/ppermute | solution.py:183
  92.4 1.3 shard_map.72
  94.6 2.3 %shard_map.69 = bf16[160,256]{1,0:T(8,128)(2,1)S(1)} custom-call(bf16[160,7168]{1,0:T(8,128)(2,1)S(1)} %pad_maximum_fusion.3.rows_ref, bf16[7168,256]{1,0:T(8,128)(2,1)S(1)} %copy-done, bf16[7168,256]{1,0:T(8,128)(2,1)S(1)} %copy-done.1), custom_call_target="tpu_custom_call" | custom-call | tf_op jit(solution)/shard_map/pallas_call | solution.py:103
  97.2 1.3 shard_map.66
  98.5 1.3 shard_map.70
  99.8 9.5 %collective-permute-done.23 = bf16[80,3584]{1,0:T(8,128)(2,1)S(1)} collective-permute-done((bf16[80,3584]{1,0:T(8,128)(2,1)S(1)}, bf16[80,3584]{1,0:T(8,128)(2,1)S(1)}, u32[]{:S(2)}, u32[]{:S(2)}) %collective-permute-start.23) | collective-permute-done | bytes 573472 | tf_op jit(solution)/shard_map/ppermute | solution.py:183
  110.2 13.9 %collective-permute-done.25 = bf16[80,3584]{1,0:T(8,128)(2,1)S(1)} collective-permute-done((bf16[80,3584]{1,0:T(8,128)(2,1)S(1)}, bf16[80,3584]{1,0:T(8,128)(2,1)S(1)}, u32[]{:S(2)}, u32[]{:S(2)}) %collective-permute-start.25) | collective-permute-done | bytes 573472 | tf_op jit(solution)/shard_map/ppermute | solution.py:183
  125.0 13.0 %collective-permute-done.26 = bf16[80,3584]{1,0:T(8,128)(2,1)S(1)} collective-permute-done((bf16[80,3584]{1,0:T(8,128)(2,1)S(1)}, bf16[80,3584]{1,0:T(8,128)(2,1)S(1)}, u32[]{:S(2)}, u32[]{:S(2)}) %collective-permute-start.26) | collective-permute-done | bytes 573472 | tf_op jit(solution)/shard_map/ppermute | solution.py:183
  138.2 12.7 %collective-permute-done.28 = bf16[80,3584]{1,0:T(8,128)(2,1)S(1)} collective-permute-done((bf16[80,3584]{1,0:T(8,128)(2,1)S(1)}, bf16[80,3584]{1,0:T(8,128)(2,1)S(1)}, u32[]{:S(2)}, u32[]{:S(2)}) %collective-permute-start.28) | collective-permute-done | bytes 573472 | tf_op jit(solution)/shard_map/ppermute | solution.py:178
  150.9 2.0 %fusion = f32[256,3584]{1,0:T(8,128)S(1)} fusion(bf16[80,3584]{1,0:T(8,128)(2,1)S(1)} %collective-permute-done.28, bf16[80,3584]{1,0:T(8,128)(2,1)S(1)} %collective-permute-done.27, bf16[80,3584]{1,0:T(8,128)(2,1)S(1)} %collective-permute-done.24, bf16[80,3584]{1,0:T(8,128)(2,1)S(1)} %add_convert_fusion.2, bf16[128,280]{1,0:T(8,128)(2,1)} %bitcast.11, ...), kind=kOutput, calls=%fused_computation.5 | convolution fusion | flops 597032960 | bytes 6117376 | tf_op jit(solution)/shard_map/dot_general | solution.py:294
  153.3 1.8 %collective-permute-done.29 = bf16[64,3584]{1,0:T(8,128)(2,1)S(1)} collective-permute-done((bf16[64,3584]{1,0:T(8,128)(2,1)S(1)}, bf16[64,3584]{1,0:T(8,128)(2,1)S(1)}, u32[]{:S(2)}, u32[]{:S(2)}) %collective-permute-start.29) | collective-permute-done | bytes 458784 | tf_op jit(solution)/shard_map/ppermute | solution.py:186
  (105 shorter events, 24.0 us)
Async XLA Ops:
  3.4 20.3 %collective-permute-start.2 = (bf16[40,7168]{1,0:T(8,128)(2,1)S(1)}, bf16[40,7168]{1,0:T(8,128)(2,1)S(1)}, u32[]{:S(2)}, u32[]{:S(2)}) collective-permute-start(bf16[40,7168]{1,0:T(8,128)(2,1)S(1)} %get-tuple-element.17), channel_id=1, source_target_pairs={{0,2},{2,0},{4,6},{6,4},{8,10},{10,8},{12,14},{14,12},{1,3},{3,1},... | collective-permute-start | bytes 1720328 | tf_op jit(solution)/shard_map/ppermute | solution.py:183
  6.4 19.3 %collective-permute-start.1 = (bf16[40,7168]{1,0:T(8,128)(2,1)S(1)}, bf16[40,7168]{1,0:T(8,128)(2,1)}, u32[]{:S(2)}, u32[]{:S(2)}) collective-permute-start(bf16[40,7168]{1,0:T(8,128)(2,1)S(1)} %get-tuple-element.17), channel_id=1, source_target_pairs={{0,1},{1,0},{2,3},{3,2},{4,5},{5,4},{6,7},{7,6},{8,9},{9,8},{10,11... | collective-permute-start | bytes 1720328 | tf_op jit(solution)/shard_map/ppermute | solution.py:186
  6.5 17.2 %collective-permute-start.6 = (bf16[40,7168]{1,0:T(8,128)(2,1)S(1)}, bf16[40,7168]{1,0:T(8,128)(2,1)S(1)}, u32[]{:S(2)}, u32[]{:S(2)}) collective-permute-start(bf16[40,7168]{1,0:T(8,128)(2,1)S(1)} %get-tuple-element.22), channel_id=1, source_target_pairs={{0,4},{2,6},{4,8},{6,10},{8,12},{10,14},{12,0},{14,2},{1,5},{3,7},... | collective-permute-start | bytes 1720328 | tf_op jit(solution)/shard_map/ppermute | solution.py:178
  13.3 124.9 %collective-permute-start = (bf16[128,320]{1,0:T(8,128)(2,1)}, bf16[128,320]{1,0:T(8,128)(2,1)}, u32[]{:S(2)}, u32[]{:S(2)}) collective-permute-start(bf16[128,320]{1,0:T(8,128)(2,1)} %pad_maximum_fusion.5), channel_id=1, source_target_pairs={{0,1},{1,0},{2,3},{3,2},{4,5},{5,4},{6,7},{7,6},{8,9},{9,8},{10,11... | collective-permute-start | bytes 245768 | tf_op jit(solution)/shard_map/ppermute | solution.py:186
  16.0 45.1 %collective-permute-start.5 = (bf16[256,3584]{1,0:T(8,128)(2,1)S(1)}, bf16[256,3584]{1,0:T(8,128)(2,1)S(1)}, u32[]{:S(2)}, u32[]{:S(2)}) collective-permute-start(bf16[256,3584]{1,0:T(8,128)(2,1)S(1)} %get-tuple-element.30), channel_id=1, source_target_pairs={{0,1},{1,0},{2,3},{3,2},{4,5},{5,4},{6,7},{7,6},{8,9},{9,8},{10,11... | collective-permute-start | bytes 5505032 | tf_op jit(solution)/shard_map/ppermute | solution.py:186
  23.7 2.5 %collective-permute-start.3 = (bf16[40,7168]{1,0:T(8,128)(2,1)S(1)}, bf16[40,7168]{1,0:T(8,128)(2,1)S(1)}, u32[]{:S(2)}, u32[]{:S(2)}) collective-permute-start(bf16[40,7168]{1,0:T(8,128)(2,1)S(1)} %collective-permute-done.2), channel_id=1, source_target_pairs={{0,1},{1,0},{2,3},{3,2},{4,5},{5,4},{6,7},{7,6},{8,9},{9,8},{10,11... | collective-permute-start | bytes 1720328 | tf_op jit(solution)/shard_map/ppermute | solution.py:186
  23.9 15.4 %collective-permute-start.7 = (bf16[40,7168]{1,0:T(8,128)(2,1)S(1)}, bf16[40,7168]{1,0:T(8,128)(2,1)S(1)}, u32[]{:S(2)}, u32[]{:S(2)}) collective-permute-start(bf16[40,7168]{1,0:T(8,128)(2,1)S(1)} %add_convert_fusion.9), channel_id=1, source_target_pairs={{0,12},{2,14},{4,0},{6,2},{8,4},{10,6},{12,8},{14,10},{1,13},{3,15... | collective-permute-start | bytes 1720328 | tf_op jit(solution)/shard_map/ppermute | solution.py:178
  25.7 15.1 %collective-permute-start.11 = (bf16[40,7168]{1,0:T(8,128)(2,1)S(1)}, bf16[40,7168]{1,0:T(8,128)(2,1)S(1)}, u32[]{:S(2)}, u32[]{:S(2)}) collective-permute-start(bf16[40,7168]{1,0:T(8,128)(2,1)S(1)} %collective-permute-done.6), channel_id=1, source_target_pairs={{0,2},{2,0},{4,6},{6,4},{8,10},{10,8},{12,14},{14,12},{1,3},{3,1},... | collective-permute-start | bytes 1720328 | tf_op jit(solution)/shard_map/ppermute | solution.py:183
  26.2 15.1 %collective-permute-start.10 = (bf16[40,7168]{1,0:T(8,128)(2,1)S(1)}, bf16[40,7168]{1,0:T(8,128)(2,1)S(1)}, u32[]{:S(2)}, u32[]{:S(2)}) collective-permute-start(bf16[40,7168]{1,0:T(8,128)(2,1)S(1)} %collective-permute-done.6), channel_id=1, source_target_pairs={{0,1},{1,0},{2,3},{3,2},{4,5},{5,4},{6,7},{7,6},{8,9},{9,8},{10,11... | collective-permute-start | bytes 1720328 | tf_op jit(solution)/shard_map/ppermute | solution.py:186
  40.9 18.8 %collective-permute-start.8 = (bf16[24,7168]{1,0:T(8,128)(2,1)S(1)}, bf16[24,7168]{1,0:T(8,128)(2,1)S(1)}, u32[]{:S(2)}, u32[]{:S(2)}) collective-permute-start(bf16[24,7168]{1,0:T(8,128)(2,1)S(1)} %add_convert_fusion.10), channel_id=1, source_target_pairs={{0,8},{2,10},{4,12},{6,14},{8,0},{10,2},{12,4},{14,6},{1,9},{3,11}... | collective-permute-start | bytes 1032200 | tf_op jit(solution)/shard_map/ppermute | solution.py:178
  41.4 36.4 %collective-permute-start.20 = (bf16[40,7168]{1,0:T(8,128)(2,1)S(1)}, bf16[40,7168]{1,0:T(8,128)(2,1)S(1)}, u32[]{:S(2)}, u32[]{:S(2)}) collective-permute-start(bf16[40,7168]{1,0:T(8,128)(2,1)S(1)} %collective-permute-done.7), channel_id=1, source_target_pairs={{0,2},{2,0},{4,6},{6,4},{8,10},{10,8},{12,14},{14,12},{1,3},{3,1},... | collective-permute-start | bytes 1720328 | tf_op jit(solution)/shard_map/ppermute | solution.py:183
  42.8 36.4 %collective-permute-start.19 = (bf16[40,7168]{1,0:T(8,128)(2,1)S(1)}, bf16[40,7168]{1,0:T(8,128)(2,1)S(1)}, u32[]{:S(2)}, u32[]{:S(2)}) collective-permute-start(bf16[40,7168]{1,0:T(8,128)(2,1)S(1)} %collective-permute-done.7), channel_id=1, source_target_pairs={{0,1},{1,0},{2,3},{3,2},{4,5},{5,4},{6,7},{7,6},{8,9},{9,8},{10,11... | collective-permute-start | bytes 1720328 | tf_op jit(solution)/shard_map/ppermute | solution.py:186
  62.6 15.1 %collective-permute-start.14 = (bf16[80,3584]{1,0:T(8,128)(2,1)S(1)}, bf16[80,3584]{1,0:T(8,128)(2,1)S(1)}, u32[]{:S(2)}, u32[]{:S(2)}) collective-permute-start(bf16[80,3584]{1,0:T(8,128)(2,1)S(1)} %get-tuple-element.23), channel_id=1, source_target_pairs={{0,2},{2,0},{4,6},{6,4},{8,10},{10,8},{12,14},{14,12},{1,3},{3,1},... | collective-permute-start | bytes 1720328 | tf_op jit(solution)/shard_map/ppermute | solution.py:183
  63.2 14.5 %collective-permute-start.9 = (bf16[16,7168]{1,0:T(8,128)(2,1)S(1)}, bf16[16,7168]{1,0:T(8,128)(2,1)S(1)}, u32[]{:S(2)}, u32[]{:S(2)}) collective-permute-start(bf16[16,7168]{1,0:T(8,128)(2,1)S(1)} %add_convert_fusion.11), channel_id=1, source_target_pairs={{0,8},{2,10},{4,12},{6,14},{8,0},{10,2},{12,4},{14,6},{1,9},{3,11}... | collective-permute-start | bytes 688136 | tf_op jit(solution)/shard_map/ppermute | solution.py:178
  78.0 14.3 %collective-permute-start.16 = (bf16[40,7168]{1,0:T(8,128)(2,1)S(1)}, bf16[40,7168]{1,0:T(8,128)(2,1)S(1)}, u32[]{:S(2)}, u32[]{:S(2)}) collective-permute-start(bf16[40,7168]{1,0:T(8,128)(2,1)S(1)} %get-tuple-element.52), channel_id=1, source_target_pairs={{0,2},{2,0},{4,6},{6,4},{8,10},{10,8},{12,14},{14,12},{1,3},{3,1},... | collective-permute-start | bytes 1720328 | tf_op jit(solution)/shard_map/ppermute | solution.py:183
  78.5 15.9 %collective-permute-start.15 = (bf16[40,7168]{1,0:T(8,128)(2,1)S(1)}, bf16[40,7168]{1,0:T(8,128)(2,1)S(1)}, u32[]{:S(2)}, u32[]{:S(2)}) collective-permute-start(bf16[40,7168]{1,0:T(8,128)(2,1)S(1)} %get-tuple-element.52), channel_id=1, source_target_pairs={{0,1},{1,0},{2,3},{3,2},{4,5},{5,4},{6,7},{7,6},{8,9},{9,8},{10,11... | collective-permute-start | bytes 1720328 | tf_op jit(solution)/shard_map/ppermute | solution.py:186
  78.5 2.8 %collective-permute-start.21 = (bf16[40,7168]{1,0:T(8,128)(2,1)S(1)}, bf16[40,7168]{1,0:T(8,128)(2,1)S(1)}, u32[]{:S(2)}, u32[]{:S(2)}) collective-permute-start(bf16[40,7168]{1,0:T(8,128)(2,1)S(1)} %get-tuple-element.51), channel_id=1, source_target_pairs={{0,1},{1,0},{2,3},{3,2},{4,5},{5,4},{6,7},{7,6},{8,9},{9,8},{10,11... | collective-permute-start | bytes 1720328 | tf_op jit(solution)/shard_map/ppermute | solution.py:186
  79.2 20.6 %collective-permute-start.24 = (bf16[80,3584]{1,0:T(8,128)(2,1)S(1)}, bf16[80,3584]{1,0:T(8,128)(2,1)S(1)}, u32[]{:S(2)}, u32[]{:S(2)}) collective-permute-start(bf16[80,3584]{1,0:T(8,128)(2,1)S(1)} %add_convert_fusion.5), channel_id=1, source_target_pairs={{0,12},{2,14},{4,0},{6,2},{8,4},{10,6},{12,8},{14,10},{1,13},{3,15... | collective-permute-start | bytes 1720328 | tf_op jit(solution)/shard_map/ppermute | solution.py:178
  83.8 8.6 %collective-permute-start.22 = (bf16[160,256]{1,0:T(8,128)(2,1)S(1)}, bf16[160,256]{1,0:T(8,128)(2,1)S(1)}, u32[]{:S(2)}, u32[]{:S(2)}) collective-permute-start(bf16[160,256]{1,0:T(8,128)(2,1)S(1)} %shard_map.71), channel_id=1, source_target_pairs={{0,1},{1,0},{2,3},{3,2},{4,5},{5,4},{6,7},{7,6},{8,9},{9,8},{10,11... | collective-permute-start | bytes 245768 | tf_op jit(solution)/shard_map/ppermute | solution.py:186
  93.9 15.4 %collective-permute-start.23 = (bf16[80,3584]{1,0:T(8,128)(2,1)S(1)}, bf16[80,3584]{1,0:T(8,128)(2,1)S(1)}, u32[]{:S(2)}, u32[]{:S(2)}) collective-permute-start(bf16[80,3584]{1,0:T(8,128)(2,1)S(1)} %add_convert_fusion.6), channel_id=1, source_target_pairs={{0,2},{2,0},{4,6},{6,4},{8,10},{10,8},{12,14},{14,12},{1,3},{3,1},... | collective-permute-start | bytes 1720328 | tf_op jit(solution)/shard_map/ppermute | solution.py:183
  109.4 14.7 %collective-permute-start.25 = (bf16[80,3584]{1,0:T(8,128)(2,1)S(1)}, bf16[80,3584]{1,0:T(8,128)(2,1)S(1)}, u32[]{:S(2)}, u32[]{:S(2)}) collective-permute-start(bf16[80,3584]{1,0:T(8,128)(2,1)S(1)} %add_convert_fusion.4), channel_id=1, source_target_pairs={{0,2},{2,0},{4,6},{6,4},{8,10},{10,8},{12,14},{14,12},{1,3},{3,1},... | collective-permute-start | bytes 1720328 | tf_op jit(solution)/shard_map/ppermute | solution.py:183
  110.2 28.0 %collective-permute-start.27 = (bf16[80,3584]{1,0:T(8,128)(2,1)S(1)}, bf16[80,3584]{1,0:T(8,128)(2,1)S(1)}, u32[]{:S(2)}, u32[]{:S(2)}) collective-permute-start(bf16[80,3584]{1,0:T(8,128)(2,1)S(1)} %add_convert_fusion.1), channel_id=1, source_target_pairs={{0,4},{2,6},{4,8},{6,10},{8,12},{10,14},{12,0},{14,2},{1,5},{3,7},... | collective-permute-start | bytes 1720328 | tf_op jit(solution)/shard_map/ppermute | solution.py:178
  124.3 13.8 %collective-permute-start.26 = (bf16[80,3584]{1,0:T(8,128)(2,1)S(1)}, bf16[80,3584]{1,0:T(8,128)(2,1)S(1)}, u32[]{:S(2)}, u32[]{:S(2)}) collective-permute-start(bf16[80,3584]{1,0:T(8,128)(2,1)S(1)} %add_convert_fusion.3), channel_id=1, source_target_pairs={{0,2},{2,0},{4,6},{6,4},{8,10},{10,8},{12,14},{14,12},{1,3},{3,1},... | collective-permute-start | bytes 1720328 | tf_op jit(solution)/shard_map/ppermute | solution.py:183
  125.0 25.9 %collective-permute-start.28 = (bf16[80,3584]{1,0:T(8,128)(2,1)S(1)}, bf16[80,3584]{1,0:T(8,128)(2,1)S(1)}, u32[]{:S(2)}, u32[]{:S(2)}) collective-permute-start(bf16[80,3584]{1,0:T(8,128)(2,1)S(1)} %add_convert_fusion), channel_id=1, source_target_pairs={{0,8},{2,10},{4,12},{6,14},{8,0},{10,2},{12,4},{14,6},{1,9},{3,11}... | collective-permute-start | bytes 1720328 | tf_op jit(solution)/shard_map/ppermute | solution.py:178
  (10 other events, 29.8 us)

commit v3 on v2

--- a/solution.py
+++ b/solution.py
@@ -8,16 +8,18 @@
 from jax.sharding import PartitionSpec as P
 
 SLICES = 4
-SPLIT = True
+SPLIT = False
+HALVED = ()
 FIRST = (1, -1)
 GATES = {
-    "a0": ("b3",),
-    "a2": ("o3",),
-    "a3": ("b2", "h1",),
-    "c2": ("b1",),
+    "a0": ("b1",),
+    "a2": ("n0",),
+    "a3": ("h1",),
+    "c3": ("b1",),
+    "h3": ("b2", "h2",),
     "y3": ("b1",),
     "z2": ("w1",),
-    "z3": ("o0", "w2",),
+    "z3": ("w2",),
 }
 
 
@@ -74,69 +76,43 @@
     )(home.reshape(1), expert_ids.T, tokens)
 
 
-def hidden_kernel(steps, rows_ref, gate_ref, up_ref, hidden_ref, gate_sum, up_sum):
-    step = pl.program_id(0)
+def hidden_kernel(rows_ref, gate_ref, up_ref, hidden_ref):
     rows = rows_ref[...]
     gate = jnp.dot(rows, gate_ref[...], preferred_element_type=jnp.float32)
     up = jnp.dot(rows, up_ref[...], preferred_element_type=jnp.float32)
-
-    @pl.when(step == 0)
-    def _():
-        gate_sum[...] = gate
-        up_sum[...] = up
-
-    @pl.when(step > 0)
-    def _():
-        gate_sum[...] += gate
-        up_sum[...] += up
-
-    @pl.when(step == steps - 1)
-    def _():
-        value = gate_sum[...]
-        hidden_ref[...] = (value / (1.0 + jnp.exp(-value)) * up_sum[...]).astype(jnp.bfloat16)
-
-
-def hidden_of(rows, gate_weight, up_weight, steps=4):
-    count, width = rows.shape
-    units = gate_weight.shape[1]
-    depth = width // steps
+    hidden_ref[...] = (gate / (1.0 + jnp.exp(-gate)) * up).astype(jnp.bfloat16)
+
+
+def hidden_of(rows, gate_weight, up_weight):
+    vmem = pl.BlockSpec(memory_space=pltpu.VMEM)
     return pl.pallas_call(
-        functools.partial(hidden_kernel, steps),
-        grid=(steps,),
-        in_specs=[
-            pl.BlockSpec((count, depth), lambda i: (0, i)),
-            pl.BlockSpec((depth, units), lambda i: (i, 0)),
-            pl.BlockSpec((depth, units), lambda i: (i, 0)),
-        ],
-        out_specs=pl.BlockSpec((count, units), lambda i: (0, 0)),
-        out_shape=jax.ShapeDtypeStruct((count, units), jnp.bfloat16),
-        scratch_shapes=[pltpu.VMEM((count, units), jnp.float32)] * 2,
-        compiler_params=pltpu.CompilerParams(vmem_limit_bytes=16 << 20),
+        hidden_kernel,
+        in_specs=[vmem] * 3,
+        out_specs=vmem,
+        out_shape=jax.ShapeDtypeStruct((rows.shape[0], gate_weight.shape[1]), jnp.bfloat16),
+        compiler_params=pltpu.CompilerParams(vmem_limit_bytes=24 << 20),
         cost_estimate=FREE,
     )(rows, gate_weight, up_weight)
 
 
-def down_kernel(hidden_ref, down_ref, near_ref, away_ref):
+def down_kernel(hidden_ref, down_ref, *made_refs):
     made = jnp.dot(hidden_ref[...], down_ref[...], preferred_element_type=jnp.float32)
-    half = near_ref.shape[0]
-    near_ref[...] = made[:half].astype(jnp.bfloat16)
-    away_ref[...] = made[half:].astype(jnp.bfloat16)
-
-
-def outputs_of(hidden, down_weight, steps=2):
-    count, units = hidden.shape
+    begin = 0
+    for made_ref in made_refs:
+        count = made_ref.shape[0]
+        made_ref[...] = made[begin : begin + count].astype(jnp.bfloat16)
+        begin += count
+
+
+def outputs_of(hidden, down_weight, counts):
+    vmem = pl.BlockSpec(memory_space=pltpu.VMEM)
     width = down_weight.shape[1]
-    columns = width // steps
     return pl.pallas_call(
         down_kernel,
-        grid=(steps,),
-        in_specs=[
-            pl.BlockSpec((count, units), lambda i: (0, 0)),
-            pl.BlockSpec((units, columns), lambda i: (0, i)),
-        ],
-        out_specs=[pl.BlockSpec((count // 2, columns), lambda i: (0, i))] * 2,
-        out_shape=[jax.ShapeDtypeStruct((count // 2, width), jnp.bfloat16)] * 2,
-        compiler_params=pltpu.CompilerParams(vmem_limit_bytes=16 << 20),
+        in_specs=[vmem] * 2,
+        out_specs=[vmem] * len(counts),
+        out_shape=[jax.ShapeDtypeStruct((n, width), jnp.bfloat16) for n in counts],
+        compiler_params=pltpu.CompilerParams(vmem_limit_bytes=24 << 20),
         cost_estimate=FREE,
     )(hidden, down_weight)
 
@@ -230,7 +206,7 @@
         found = gates(point)
         return hold(rows, *found) if found else rows
 
-    own, own_far, near, raw = {}, {}, {}, {}
+    own, own_far, near, raw, back, whole = {}, {}, {}, {}, {}, []
 
     def dispatch(k):
         if k == 0:
@@ -259,15 +235,22 @@
         flat = jnp.concatenate([own[k], own_far[k], other, swap(other)], axis=0)
         hidden = hidden_of(flat, gate_weight, up_weight)
         hidden = jnp.concatenate([hidden, turned(swap(hidden))], axis=1)
-        near[k], raw[k] = outputs_of(hidden, down_half)
-        seen["n%d" % k] = near[k]
+        parts = 2 if k in HALVED else 1
+        made = outputs_of(hidden, down_half, [2 * capacity // parts] * (2 * parts))
+        near[k], raw[k] = made[:parts], made[parts:]
+        seen["n%d" % k] = near[k][0]
 
     def merge(k):
-        seen["b%d" % k] = over(maybe_hold(raw[k], "a%d" % k))
+        back[k] = [over(maybe_hold(rows, "a%d" % k)) for rows in raw[k]]
+        seen["b%d" % k] = back[k][-1]
+        seen["B%d" % k] = back[k][0]
 
     def give_back(k):
-        total = add_rows(near[k], seen["b%d" % k])
-        seen["h%d" % k] = along(total, -order[k]) if k else total
+        totals = [add_rows(*pair) for pair in zip(near[k], back[k])]
+        if k:
+            totals = [along(maybe_hold(rows, "h%d" % k), -order[k]) for rows in totals]
+        seen["h%d" % k] = totals[-1]
+        whole.extend(zip([2 * k, 2 * k + 1], totals))
 
     for k in range(3):
         dispatch(k)
@@ -289,7 +272,7 @@
     merge(0)
     give_back(last)
     give_back(0)
-    whole = [seen["h%d" % k] for k in range(experts)]
+    whole = [rows for _, rows in sorted(whole, key=lambda item: item[0])]
     returned = jnp.concatenate(whole, axis=0)
     product = jnp.dot(all_weights, returned, preferred_element_type=jnp.float32)
     product = product.reshape(2, 2, row_count, wide)

time: 157 us -> 154 us (0.981)
  starting transfers between devices: 14.1 us -> 22 us
  Pallas kernels: 15.8 us -> 10.3 us
  waiting for transfers between devices: 109 us -> 104 us
    ppermute x7 -> x6, starting transfers between devices: 5.23 us -> 11.1 us  [along(): lax.ppermute(rows, 'expert', [(i, (i + per * step) % chips) for i in rang...]
    pallas_call x8, Pallas kernels: 14.3 us -> 8.76 us  [the longest x4 5.69 us: hidden_of(): pl.pallas_call(hidden_kernel, in_specs=[vmem] * 3, out_specs=vmem, out_sh...]
    ppermute x7 -> x6, waiting for transfers between devices: 44.1 us -> 41.1 us  [along(): lax.ppermute(rows, 'expert', [(i, (i + per * step) % chips) for i in rang...]
    ppermute x8, waiting for transfers between devices: 60.4 us -> 58.1 us  [over(): return lax.ppermute(rows, 'expert', across)]
    ppermute x8, starting transfers between devices: 6.97 us -> 9 us  [over(): return lax.ppermute(rows, 'expert', across)]
  transfers between devices with their start and end apart: 30 -> 29, of which waited for: 14 -> 14; matrix products, arithmetic and copies ran while one was open for 7% -> 7% of each run, Pallas kernels for 9% -> 6%
where the time goes in v3:
time: 154 us; the launch traced here: 153 us
  waiting for transfers between devices  104 us (68%)
  starting transfers between devices  22 us (14%)
  Pallas kernels  10.3 us (7%)
  other arithmetic  9.55 us (6%)
  local copies, waits for them, and re-layouts  4.84 us (3%)
  matrix products  2.02 us (1%)
    ppermute x8, waiting for transfers between devices, over(): return lax.ppermute(rows, 'expert', across)  58.1 us
    ppermute x6, waiting for transfers between devices, along(): lax.ppermute(rows, 'expert', [(i, (i + per * step) % chips) for i in rang...  41.1 us
    ppermute x6, starting transfers between devices, along(): lax.ppermute(rows, 'expert', [(i, (i + per * step) % chips) for i in rang...  11.1 us
    ppermute x8, starting transfers between devices, over(): return lax.ppermute(rows, 'expert', across)  9 us
    pallas_call x4, Pallas kernels, hidden_of(): pl.pallas_call(hidden_kernel, in_specs=[vmem] * 3, out_specs=vmem, out_sh...  5.69 us
    ppermute x15, waiting for transfers between devices, swap(): return lax.ppermute(rows, 'dp', [(0, 1), (1, 0)])  4.92 us
  transfers between devices with their start and end apart: 29, of which 14 were waited for; matrix products, arithmetic and copies ran while one was open for 7% of the time, Pallas kernels for 6%

profile of v3, /device:TPU:0, one launch (start us, length us, event | category | flops | bytes accessed | tf_op | source)
XLA Modules:
  0.0 153.2 jit_solution(16458886188233172739)
XLA Ops:
  1.9 1.6 %shard_map.64 = (bf16[40,7168]{1,0:T(8,128)(2,1)S(1)}, bf16[40,7168]{1,0:T(8,128)(2,1)S(1)}, bf16[40,7168]{1,0:T(8,128)(2,1)S(1)}, bf16[40,7168]{1,0:T(8,128)(2,1)S(1)}) custom-call(s32[1]{0:T(128)} %bitcast.home_ref, s32[2,64]{1,0:T(2,128)S(1)} %bitcast.11, bf16[64,7168]{1,0:T(8,128)(2,1)S(1)} %copy-done.2), custom_call_target="tpu_custom_call" | custom-call | tf_op jit(solution)/shard_map/pallas_call | solution.py:69
  3.4 3.0 %collective-permute-start.2 = (bf16[40,7168]{1,0:T(8,128)(2,1)S(1)}, bf16[40,7168]{1,0:T(8,128)(2,1)S(1)}, u32[]{:S(2)}, u32[]{:S(2)}) collective-permute-start(bf16[40,7168]{1,0:T(8,128)(2,1)S(1)} %get-tuple-element.17), channel_id=1, source_target_pairs={{0,2},{2,0},{4,6},{6,4},{8,10},{10,8},{12,14},{14,12},{1,3},{3,1},... | collective-permute-start | bytes 1720328 | tf_op jit(solution)/shard_map/ppermute | solution.py:159
  6.5 1.6 %collective-permute-start.6 = (bf16[40,7168]{1,0:T(8,128)(2,1)S(1)}, bf16[40,7168]{1,0:T(8,128)(2,1)S(1)}, u32[]{:S(2)}, u32[]{:S(2)}) collective-permute-start(bf16[40,7168]{1,0:T(8,128)(2,1)S(1)} %get-tuple-element.20), channel_id=1, source_target_pairs={{0,4},{2,6},{4,8},{6,10},{8,12},{10,14},{12,0},{14,2},{1,5},{3,7},... | collective-permute-start | bytes 1720328 | tf_op jit(solution)/shard_map/ppermute | solution.py:154
  13.5 2.4 %constant_dynamic-slice_fusion = (bf16[256,3584]{1,0:T(8,128)(2,1)S(1)}, bf16[256,3584]{1,0:T(8,128)(2,1)S(1)}) fusion(bf16[256,7168]{1,0:T(8,128)(2,1)} %param.11, s32[]{:T(128)S(6)} %select_n.40, s32[]{:T(128)S(6)} %select_n.41), kind=kLoop, calls=%fused_computation.76 | loop fusion | bytes 7340040 | tf_op jit(solution)/shard_map/dynamic_slice | solution.py:191
  16.3 7.4 %collective-permute-done.6 = bf16[40,7168]{1,0:T(8,128)(2,1)S(1)} collective-permute-done((bf16[40,7168]{1,0:T(8,128)(2,1)S(1)}, bf16[40,7168]{1,0:T(8,128)(2,1)S(1)}, u32[]{:S(2)}, u32[]{:S(2)}) %collective-permute-start.6) | collective-permute-done | bytes 573472 | tf_op jit(solution)/shard_map/ppermute | solution.py:154
  23.9 1.8 %collective-permute-start.14 = (bf16[40,7168]{1,0:T(8,128)(2,1)S(1)}, bf16[40,7168]{1,0:T(8,128)(2,1)S(1)}, u32[]{:S(2)}, u32[]{:S(2)}) collective-permute-start(bf16[40,7168]{1,0:T(8,128)(2,1)S(1)} %add_convert_fusion.8), channel_id=1, source_target_pairs={{0,12},{2,14},{4,0},{6,2},{8,4},{10,6},{12,8},{14,10},{1,13},{3,15... | collective-permute-start | bytes 1720328 | tf_op jit(solution)/shard_map/ppermute | solution.py:154
  27.5 1.5 shard_map.65
  29.0 10.4 %collective-permute-done.14 = bf16[40,7168]{1,0:T(8,128)(2,1)S(1)} collective-permute-done((bf16[40,7168]{1,0:T(8,128)(2,1)S(1)}, bf16[40,7168]{1,0:T(8,128)(2,1)S(1)}, u32[]{:S(2)}, u32[]{:S(2)}) %collective-permute-start.14) | collective-permute-done | bytes 573472 | tf_op jit(solution)/shard_map/ppermute | solution.py:154
  39.4 1.4 collective-permute-done.8
  43.0 1.5 shard_map.67
  44.7 11.8 %collective-permute-done.16 = bf16[40,7168]{1,0:T(8,128)(2,1)S(1)} collective-permute-done((bf16[40,7168]{1,0:T(8,128)(2,1)S(1)}, bf16[40,7168]{1,0:T(8,128)(2,1)S(1)}, u32[]{:S(2)}, u32[]{:S(2)}) %collective-permute-start.16) | collective-permute-done | bytes 573472 | tf_op jit(solution)/shard_map/ppermute | solution.py:159
  63.2 1.6 %collective-permute-start.19 = (bf16[80,3584]{1,0:T(8,128)(2,1)S(1)}, bf16[80,3584]{1,0:T(8,128)(2,1)S(1)}, u32[]{:S(2)}, u32[]{:S(2)}) collective-permute-start(bf16[80,3584]{1,0:T(8,128)(2,1)S(1)} %add_convert_fusion.7), channel_id=1, source_target_pairs={{0,2},{2,0},{4,6},{6,4},{8,10},{10,8},{12,14},{14,12},{1,3},{3,1},... | collective-permute-start | bytes 1720328 | tf_op jit(solution)/shard_map/ppermute | solution.py:159
  64.8 9.2 %collective-permute-done.11 = bf16[80,3584]{1,0:T(8,128)(2,1)S(1)} collective-permute-done((bf16[80,3584]{1,0:T(8,128)(2,1)S(1)}, bf16[80,3584]{1,0:T(8,128)(2,1)S(1)}, u32[]{:S(2)}, u32[]{:S(2)}) %collective-permute-start.11) | collective-permute-done | bytes 573472 | tf_op jit(solution)/shard_map/ppermute | solution.py:159
  74.9 2.9 %collective-permute-start.13 = (bf16[80,3584]{1,0:T(8,128)(2,1)S(1)}, bf16[80,3584]{1,0:T(8,128)(2,1)S(1)}, u32[]{:S(2)}, u32[]{:S(2)}) collective-permute-start(bf16[80,3584]{1,0:T(8,128)(2,1)S(1)} %add_convert_fusion.9), channel_id=1, source_target_pairs={{0,12},{2,14},{4,0},{6,2},{8,4},{10,6},{12,8},{14,10},{1,13},{3,15... | collective-permute-start | bytes 1720328 | tf_op jit(solution)/shard_map/ppermute | solution.py:154
  77.7 19.9 %collective-permute-done.23 = bf16[40,7168]{1,0:T(8,128)(2,1)S(1)} collective-permute-done((bf16[40,7168]{1,0:T(8,128)(2,1)S(1)}, bf16[40,7168]{1,0:T(8,128)(2,1)S(1)}, u32[]{:S(2)}, u32[]{:S(2)}) %collective-permute-start.23) | collective-permute-done | bytes 573472 | tf_op jit(solution)/shard_map/ppermute | solution.py:159
  97.9 3.3 %collective-permute-start.20 = (bf16[80,3584]{1,0:T(8,128)(2,1)S(1)}, bf16[80,3584]{1,0:T(8,128)(2,1)S(1)}, u32[]{:S(2)}, u32[]{:S(2)}) collective-permute-start(bf16[80,3584]{1,0:T(8,128)(2,1)S(1)} %add_convert_fusion.6), channel_id=1, source_target_pairs={{0,4},{2,6},{4,8},{6,10},{8,12},{10,14},{12,0},{14,2},{1,5},{3,7},... | collective-permute-start | bytes 1720328 | tf_op jit(solution)/shard_map/ppermute | solution.py:154
  101.4 1.4 shard_map.71
  105.7 1.6 %collective-permute-start.12 = (bf16[80,3584]{1,0:T(8,128)(2,1)S(1)}, bf16[80,3584]{1,0:T(8,128)(2,1)S(1)}, u32[]{:S(2)}, u32[]{:S(2)}) collective-permute-start(bf16[80,3584]{1,0:T(8,128)(2,1)S(1)} %add_convert_fusion.11), channel_id=1, source_target_pairs={{0,2},{2,0},{4,6},{6,4},{8,10},{10,8},{12,14},{14,12},{1,3},{3,1},... | collective-permute-start | bytes 1720328 | tf_op jit(solution)/shard_map/ppermute | solution.py:159
  107.3 8.0 %collective-permute-done.20 = bf16[80,3584]{1,0:T(8,128)(2,1)S(1)} collective-permute-done((bf16[80,3584]{1,0:T(8,128)(2,1)S(1)}, bf16[80,3584]{1,0:T(8,128)(2,1)S(1)}, u32[]{:S(2)}, u32[]{:S(2)}) %collective-permute-start.20) | collective-permute-done | bytes 573472 | tf_op jit(solution)/shard_map/ppermute | solution.py:154
  115.4 5.5 %collective-permute-done.26 = bf16[80,3584]{1,0:T(8,128)(2,1)S(1)} collective-permute-done((bf16[80,3584]{1,0:T(8,128)(2,1)S(1)}, bf16[80,3584]{1,0:T(8,128)(2,1)S(1)}, u32[]{:S(2)}, u32[]{:S(2)}) %collective-permute-start.26) | collective-permute-done | bytes 573472 | tf_op jit(solution)/shard_map/ppermute | solution.py:159
  122.3 10.2 %collective-permute-done.12 = bf16[80,3584]{1,0:T(8,128)(2,1)S(1)} collective-permute-done((bf16[80,3584]{1,0:T(8,128)(2,1)S(1)}, bf16[80,3584]{1,0:T(8,128)(2,1)S(1)}, u32[]{:S(2)}, u32[]{:S(2)}) %collective-permute-start.12) | collective-permute-done | bytes 573472 | tf_op jit(solution)/shard_map/ppermute | solution.py:159
  132.6 15.2 %collective-permute-done.27 = bf16[80,3584]{1,0:T(8,128)(2,1)S(1)} collective-permute-done((bf16[80,3584]{1,0:T(8,128)(2,1)S(1)}, bf16[80,3584]{1,0:T(8,128)(2,1)S(1)}, u32[]{:S(2)}, u32[]{:S(2)}) %collective-permute-start.27) | collective-permute-done | bytes 573472 | tf_op jit(solution)/shard_map/ppermute | solution.py:154
  147.9 2.0 %fusion = f32[256,3584]{1,0:T(8,128)S(1)} fusion(bf16[80,3584]{1,0:T(8,128)(2,1)S(1)} %collective-permute-done.27, bf16[80,3584]{1,0:T(8,128)(2,1)S(1)} %collective-permute-done.20, bf16[80,3584]{1,0:T(8,128)(2,1)S(1)} %collective-permute-done.13, bf16[80,3584]{1,0:T(8,128)(2,1)S(1)} %add_convert_fusion.10, bf16[128,280]{1,0:T(8,128)(2,1)} %bitcast.10, ...), kind=kOutput, calls=%fused_computation.5 | convolution fusion | flops 597032960 | bytes 6117376 | tf_op jit(solution)/shard_map/dot_general | solution.py:277
  150.3 1.8 %collective-permute-done.28 = bf16[64,3584]{1,0:T(8,128)(2,1)S(1)} collective-permute-done((bf16[64,3584]{1,0:T(8,128)(2,1)S(1)}, bf16[64,3584]{1,0:T(8,128)(2,1)S(1)}, u32[]{:S(2)}, u32[]{:S(2)}) %collective-permute-start.28) | collective-permute-done | bytes 458784 | tf_op jit(solution)/shard_map/ppermute | solution.py:162
  (101 shorter events, 25.8 us)
Async XLA Ops:
  3.4 20.3 %collective-permute-start.2 = (bf16[40,7168]{1,0:T(8,128)(2,1)S(1)}, bf16[40,7168]{1,0:T(8,128)(2,1)S(1)}, u32[]{:S(2)}, u32[]{:S(2)}) collective-permute-start(bf16[40,7168]{1,0:T(8,128)(2,1)S(1)} %get-tuple-element.17), channel_id=1, source_target_pairs={{0,2},{2,0},{4,6},{6,4},{8,10},{10,8},{12,14},{14,12},{1,3},{3,1},... | collective-permute-start | bytes 1720328 | tf_op jit(solution)/shard_map/ppermute | solution.py:159
  6.5 19.3 %collective-permute-start.1 = (bf16[40,7168]{1,0:T(8,128)(2,1)S(1)}, bf16[40,7168]{1,0:T(8,128)(2,1)}, u32[]{:S(2)}, u32[]{:S(2)}) collective-permute-start(bf16[40,7168]{1,0:T(8,128)(2,1)S(1)} %get-tuple-element.17), channel_id=1, source_target_pairs={{0,1},{1,0},{2,3},{3,2},{4,5},{5,4},{6,7},{7,6},{8,9},{9,8},{10,11... | collective-permute-start | bytes 1720328 | tf_op jit(solution)/shard_map/ppermute | solution.py:162
  6.5 17.2 %collective-permute-start.6 = (bf16[40,7168]{1,0:T(8,128)(2,1)S(1)}, bf16[40,7168]{1,0:T(8,128)(2,1)S(1)}, u32[]{:S(2)}, u32[]{:S(2)}) collective-permute-start(bf16[40,7168]{1,0:T(8,128)(2,1)S(1)} %get-tuple-element.20), channel_id=1, source_target_pairs={{0,4},{2,6},{4,8},{6,10},{8,12},{10,14},{12,0},{14,2},{1,5},{3,7},... | collective-permute-start | bytes 1720328 | tf_op jit(solution)/shard_map/ppermute | solution.py:154
  13.3 119.3 %collective-permute-start = (bf16[128,320]{1,0:T(8,128)(2,1)}, bf16[128,320]{1,0:T(8,128)(2,1)}, u32[]{:S(2)}, u32[]{:S(2)}) collective-permute-start(bf16[128,320]{1,0:T(8,128)(2,1)} %pad_maximum_fusion.5), channel_id=1, source_target_pairs={{0,1},{1,0},{2,3},{3,2},{4,5},{5,4},{6,7},{7,6},{8,9},{9,8},{10,11... | collective-permute-start | bytes 245768 | tf_op jit(solution)/shard_map/ppermute | solution.py:162
  16.0 41.1 %collective-permute-start.5 = (bf16[256,3584]{1,0:T(8,128)(2,1)S(1)}, bf16[256,3584]{1,0:T(8,128)(2,1)S(1)}, u32[]{:S(2)}, u32[]{:S(2)}) collective-permute-start(bf16[256,3584]{1,0:T(8,128)(2,1)S(1)} %get-tuple-element.30), channel_id=1, source_target_pairs={{0,1},{1,0},{2,3},{3,2},{4,5},{5,4},{6,7},{7,6},{8,9},{9,8},{10,11... | collective-permute-start | bytes 5505032 | tf_op jit(solution)/shard_map/ppermute | solution.py:162
  23.7 2.5 %collective-permute-start.3 = (bf16[40,7168]{1,0:T(8,128)(2,1)S(1)}, bf16[40,7168]{1,0:T(8,128)(2,1)S(1)}, u32[]{:S(2)}, u32[]{:S(2)}) collective-permute-start(bf16[40,7168]{1,0:T(8,128)(2,1)S(1)} %collective-permute-done.2), channel_id=1, source_target_pairs={{0,1},{1,0},{2,3},{3,2},{4,5},{5,4},{6,7},{7,6},{8,9},{9,8},{10,11... | collective-permute-start | bytes 1720328 | tf_op jit(solution)/shard_map/ppermute | solution.py:162
  23.9 15.4 %collective-permute-start.14 = (bf16[40,7168]{1,0:T(8,128)(2,1)S(1)}, bf16[40,7168]{1,0:T(8,128)(2,1)S(1)}, u32[]{:S(2)}, u32[]{:S(2)}) collective-permute-start(bf16[40,7168]{1,0:T(8,128)(2,1)S(1)} %add_convert_fusion.8), channel_id=1, source_target_pairs={{0,12},{2,14},{4,0},{6,2},{8,4},{10,6},{12,8},{14,10},{1,13},{3,15... | collective-permute-start | bytes 1720328 | tf_op jit(solution)/shard_map/ppermute | solution.py:154
  25.7 15.1 %collective-permute-start.8 = (bf16[40,7168]{1,0:T(8,128)(2,1)S(1)}, bf16[40,7168]{1,0:T(8,128)(2,1)S(1)}, u32[]{:S(2)}, u32[]{:S(2)}) collective-permute-start(bf16[40,7168]{1,0:T(8,128)(2,1)S(1)} %collective-permute-done.6), channel_id=1, source_target_pairs={{0,2},{2,0},{4,6},{6,4},{8,10},{10,8},{12,14},{14,12},{1,3},{3,1},... | collective-permute-start | bytes 1720328 | tf_op jit(solution)/shard_map/ppermute | solution.py:159
  26.2 15.1 %collective-permute-start.7 = (bf16[40,7168]{1,0:T(8,128)(2,1)S(1)}, bf16[40,7168]{1,0:T(8,128)(2,1)S(1)}, u32[]{:S(2)}, u32[]{:S(2)}) collective-permute-start(bf16[40,7168]{1,0:T(8,128)(2,1)S(1)} %collective-permute-done.6), channel_id=1, source_target_pairs={{0,1},{1,0},{2,3},{3,2},{4,5},{5,4},{6,7},{7,6},{8,9},{9,8},{10,11... | collective-permute-start | bytes 1720328 | tf_op jit(solution)/shard_map/ppermute | solution.py:162
  40.9 33.1 %collective-permute-start.21 = (bf16[40,7168]{1,0:T(8,128)(2,1)S(1)}, bf16[40,7168]{1,0:T(8,128)(2,1)S(1)}, u32[]{:S(2)}, u32[]{:S(2)}) collective-permute-start(bf16[40,7168]{1,0:T(8,128)(2,1)S(1)} %add_convert_fusion.5), channel_id=1, source_target_pairs={{0,8},{2,10},{4,12},{6,14},{8,0},{10,2},{12,4},{14,6},{1,9},{3,11}... | collective-permute-start | bytes 1720328 | tf_op jit(solution)/shard_map/ppermute | solution.py:154
  41.4 15.1 %collective-permute-start.16 = (bf16[40,7168]{1,0:T(8,128)(2,1)S(1)}, bf16[40,7168]{1,0:T(8,128)(2,1)S(1)}, u32[]{:S(2)}, u32[]{:S(2)}) collective-permute-start(bf16[40,7168]{1,0:T(8,128)(2,1)S(1)} %collective-permute-done.14), channel_id=1, source_target_pairs={{0,2},{2,0},{4,6},{6,4},{8,10},{10,8},{12,14},{14,12},{1,3},{3,1},... | collective-permute-start | bytes 1720328 | tf_op jit(solution)/shard_map/ppermute | solution.py:159
  44.5 12.1 %collective-permute-start.10 = (bf16[160,256]{1,0:T(8,128)(2,1)S(1)}, bf16[160,256]{1,0:T(8,128)(2,1)S(1)}, u32[]{:S(2)}, u32[]{:S(2)}) collective-permute-start(bf16[160,256]{1,0:T(8,128)(2,1)S(1)} %shard_map.67), channel_id=1, source_target_pairs={{0,1},{1,0},{2,3},{3,2},{4,5},{5,4},{6,7},{7,6},{8,9},{9,8},{10,11... | collective-permute-start | bytes 245768 | tf_op jit(solution)/shard_map/ppermute | solution.py:162
  56.5 2.9 %collective-permute-start.15 = (bf16[40,7168]{1,0:T(8,128)(2,1)S(1)}, bf16[40,7168]{1,0:T(8,128)(2,1)S(1)}, u32[]{:S(2)}, u32[]{:S(2)}) collective-permute-start(bf16[40,7168]{1,0:T(8,128)(2,1)S(1)} %collective-permute-done.14), channel_id=1, source_target_pairs={{0,1},{1,0},{2,3},{3,2},{4,5},{5,4},{6,7},{7,6},{8,9},{9,8},{10,11... | collective-permute-start | bytes 1720328 | tf_op jit(solution)/shard_map/ppermute | solution.py:162
  56.5 2.9 %collective-permute-start.17 = (bf16[40,7168]{1,0:T(8,128)(2,1)S(1)}, bf16[40,7168]{1,0:T(8,128)(2,1)S(1)}, u32[]{:S(2)}, u32[]{:S(2)}) collective-permute-start(bf16[40,7168]{1,0:T(8,128)(2,1)S(1)} %collective-permute-done.16), channel_id=1, source_target_pairs={{0,1},{1,0},{2,3},{3,2},{4,5},{5,4},{6,7},{7,6},{8,9},{9,8},{10,11... | collective-permute-start | bytes 1720328 | tf_op jit(solution)/shard_map/ppermute | solution.py:162
  58.1 15.9 %collective-permute-start.11 = (bf16[80,3584]{1,0:T(8,128)(2,1)S(1)}, bf16[80,3584]{1,0:T(8,128)(2,1)S(1)}, u32[]{:S(2)}, u32[]{:S(2)}) collective-permute-start(bf16[80,3584]{1,0:T(8,128)(2,1)S(1)} %get-tuple-element.21), channel_id=1, source_target_pairs={{0,2},{2,0},{4,6},{6,4},{8,10},{10,8},{12,14},{14,12},{1,3},{3,1},... | collective-permute-start | bytes 1720328 | tf_op jit(solution)/shard_map/ppermute | solution.py:159
  63.2 34.6 %collective-permute-start.19 = (bf16[80,3584]{1,0:T(8,128)(2,1)S(1)}, bf16[80,3584]{1,0:T(8,128)(2,1)S(1)}, u32[]{:S(2)}, u32[]{:S(2)}) collective-permute-start(bf16[80,3584]{1,0:T(8,128)(2,1)S(1)} %add_convert_fusion.7), channel_id=1, source_target_pairs={{0,2},{2,0},{4,6},{6,4},{8,10},{10,8},{12,14},{14,12},{1,3},{3,1},... | collective-permute-start | bytes 1720328 | tf_op jit(solution)/shard_map/ppermute | solution.py:159
  74.2 23.4 %collective-permute-start.23 = (bf16[40,7168]{1,0:T(8,128)(2,1)S(1)}, bf16[40,7168]{1,0:T(8,128)(2,1)S(1)}, u32[]{:S(2)}, u32[]{:S(2)}) collective-permute-start(bf16[40,7168]{1,0:T(8,128)(2,1)S(1)} %add_convert_fusion.4), channel_id=1, source_target_pairs={{0,2},{2,0},{4,6},{6,4},{8,10},{10,8},{12,14},{14,12},{1,3},{3,1},... | collective-permute-start | bytes 1720328 | tf_op jit(solution)/shard_map/ppermute | solution.py:159
  74.7 26.5 %collective-permute-start.22 = (bf16[40,7168]{1,0:T(8,128)(2,1)S(1)}, bf16[40,7168]{1,0:T(8,128)(2,1)S(1)}, u32[]{:S(2)}, u32[]{:S(2)}) collective-permute-start(bf16[40,7168]{1,0:T(8,128)(2,1)S(1)} %add_convert_fusion.4), channel_id=1, source_target_pairs={{0,1},{1,0},{2,3},{3,2},{4,5},{5,4},{6,7},{7,6},{8,9},{9,8},{10,11... | collective-permute-start | bytes 1720328 | tf_op jit(solution)/shard_map/ppermute | solution.py:162
  74.9 28.2 %collective-permute-start.13 = (bf16[80,3584]{1,0:T(8,128)(2,1)S(1)}, bf16[80,3584]{1,0:T(8,128)(2,1)S(1)}, u32[]{:S(2)}, u32[]{:S(2)}) collective-permute-start(bf16[80,3584]{1,0:T(8,128)(2,1)S(1)} %add_convert_fusion.9), channel_id=1, source_target_pairs={{0,12},{2,14},{4,0},{6,2},{8,4},{10,6},{12,8},{14,10},{1,13},{3,15... | collective-permute-start | bytes 1720328 | tf_op jit(solution)/shard_map/ppermute | solution.py:154
  97.7 3.5 %collective-permute-start.24 = (bf16[40,7168]{1,0:T(8,128)(2,1)S(1)}, bf16[40,7168]{1,0:T(8,128)(2,1)S(1)}, u32[]{:S(2)}, u32[]{:S(2)}) collective-permute-start(bf16[40,7168]{1,0:T(8,128)(2,1)S(1)} %add_convert_fusion.3), channel_id=1, source_target_pairs={{0,1},{1,0},{2,3},{3,2},{4,5},{5,4},{6,7},{7,6},{8,9},{9,8},{10,11... | collective-permute-start | bytes 1720328 | tf_op jit(solution)/shard_map/ppermute | solution.py:162
  97.9 17.4 %collective-permute-start.20 = (bf16[80,3584]{1,0:T(8,128)(2,1)S(1)}, bf16[80,3584]{1,0:T(8,128)(2,1)S(1)}, u32[]{:S(2)}, u32[]{:S(2)}) collective-permute-start(bf16[80,3584]{1,0:T(8,128)(2,1)S(1)} %add_convert_fusion.6), channel_id=1, source_target_pairs={{0,4},{2,6},{4,8},{6,10},{8,12},{10,14},{12,0},{14,2},{1,5},{3,7},... | collective-permute-start | bytes 1720328 | tf_op jit(solution)/shard_map/ppermute | solution.py:154
  105.1 15.9 %collective-permute-start.26 = (bf16[80,3584]{1,0:T(8,128)(2,1)S(1)}, bf16[80,3584]{1,0:T(8,128)(2,1)S(1)}, u32[]{:S(2)}, u32[]{:S(2)}) collective-permute-start(bf16[80,3584]{1,0:T(8,128)(2,1)S(1)} %add_convert_fusion.2), channel_id=1, source_target_pairs={{0,2},{2,0},{4,6},{6,4},{8,10},{10,8},{12,14},{14,12},{1,3},{3,1},... | collective-permute-start | bytes 1720328 | tf_op jit(solution)/shard_map/ppermute | solution.py:159
  105.7 26.8 %collective-permute-start.12 = (bf16[80,3584]{1,0:T(8,128)(2,1)S(1)}, bf16[80,3584]{1,0:T(8,128)(2,1)S(1)}, u32[]{:S(2)}, u32[]{:S(2)}) collective-permute-start(bf16[80,3584]{1,0:T(8,128)(2,1)S(1)} %add_convert_fusion.11), channel_id=1, source_target_pairs={{0,2},{2,0},{4,6},{6,4},{8,10},{10,8},{12,14},{14,12},{1,3},{3,1},... | collective-permute-start | bytes 1720328 | tf_op jit(solution)/shard_map/ppermute | solution.py:159
  121.1 26.8 %collective-permute-start.27 = (bf16[80,3584]{1,0:T(8,128)(2,1)S(1)}, bf16[80,3584]{1,0:T(8,128)(2,1)S(1)}, u32[]{:S(2)}, u32[]{:S(2)}) collective-permute-start(bf16[80,3584]{1,0:T(8,128)(2,1)S(1)} %add_convert_fusion), channel_id=1, source_target_pairs={{0,8},{2,10},{4,12},{6,14},{8,0},{10,2},{12,4},{14,6},{1,9},{3,11}... | collective-permute-start | bytes 1720328 | tf_op jit(solution)/shard_map/ppermute | solution.py:154
  (9 other events, 27.5 us)

commit v4 on v3

--- a/solution.py
+++ b/solution.py
@@ -12,13 +12,13 @@
 HALVED = ()
 FIRST = (1, -1)
 GATES = {
-    "a0": ("b1",),
     "a2": ("n0",),
     "a3": ("h1",),
+    "c2": ("n1",),
     "c3": ("b1",),
-    "h3": ("b2", "h2",),
+    "h3": ("h2",),
     "y3": ("b1",),
-    "z2": ("w1",),
+    "z2": ("o0", "w1",),
     "z3": ("w2",),
 }
 

time: 154 us -> 148 us (0.961)
  local copies, waits for them, and re-layouts: 4.84 us -> 9.69 us
  starting transfers between devices: 22 us -> 17.5 us
  waiting for transfers between devices: 104 us -> 100 us
    ppermute x6, waiting for transfers between devices: 41.1 us -> 36.5 us  [along(): lax.ppermute(rows, 'expert', [(i, (i + per * step) % chips) for i in rang...]
    ppermute x6, starting transfers between devices: 11.1 us -> 7.25 us  [along(): lax.ppermute(rows, 'expert', [(i, (i + per * step) % chips) for i in rang...]
    unnamed x8 -> x16, local copies, waits for them, and re-layouts: 1.87 us -> 5.06 us
    ppermute x8, waiting for transfers between devices: 58.1 us -> 59.7 us  [over(): return lax.ppermute(rows, 'expert', across)]
    dynamic_slice x1, local copies, waits for them, and re-layouts: 2.44 us -> 4.1 us  [local(): down_near = lax.dynamic_slice_in_dim(down_weight, core * wide, wide, 1)]
  transfers between devices with their start and end apart: 29 -> 29, of which waited for: 14 -> 16; matrix products, arithmetic and copies ran while one was open for 7% -> 8% of each run, Pallas kernels for 6% -> 6%
where the time goes in v4:
time: 148 us; the launch traced here: 147 us
  waiting for transfers between devices  100 us (68%)
  starting transfers between devices  17.5 us (12%)
  Pallas kernels  10.3 us (7%)
  local copies, waits for them, and re-layouts  9.69 us (7%)
  other arithmetic  8.4 us (6%)
    ppermute x8, waiting for transfers between devices, over(): return lax.ppermute(rows, 'expert', across)  59.7 us
    ppermute x6, waiting for transfers between devices, along(): lax.ppermute(rows, 'expert', [(i, (i + per * step) % chips) for i in rang...  36.5 us
    ppermute x8, starting transfers between devices, over(): return lax.ppermute(rows, 'expert', across)  8.4 us
    ppermute x6, starting transfers between devices, along(): lax.ppermute(rows, 'expert', [(i, (i + per * step) % chips) for i in rang...  7.25 us
    pallas_call x4, Pallas kernels, hidden_of(): pl.pallas_call(hidden_kernel, in_specs=[vmem] * 3, out_specs=vmem, out_sh...  5.63 us
    unnamed x16, local copies, waits for them, and re-layouts  5.06 us
    dynamic_slice x1, local copies, waits for them, and re-layouts, local(): down_near = lax.dynamic_slice_in_dim(down_weight, core * wide, wide, 1)  4.1 us
    ppermute x15, waiting for transfers between devices, swap(): return lax.ppermute(rows, 'dp', [(0, 1), (1, 0)])  3.83 us
  transfers between devices with their start and end apart: 29, of which 16 were waited for; matrix products, arithmetic and copies ran while one was open for 8% of the time, Pallas kernels for 6%

profile of v4, /device:TPU:0, one launch (start us, length us, event | category | flops | bytes accessed | tf_op | source)
XLA Modules:
  0.0 147.5 jit_solution(1651131306407345898)
XLA Ops:
  1.9 1.6 %shard_map.64 = (bf16[40,7168]{1,0:T(8,128)(2,1)S(1)}, bf16[40,7168]{1,0:T(8,128)(2,1)S(1)}, bf16[40,7168]{1,0:T(8,128)(2,1)S(1)}, bf16[40,7168]{1,0:T(8,128)(2,1)S(1)}) custom-call(s32[1]{0:T(128)} %bitcast.home_ref, s32[2,64]{1,0:T(2,128)S(1)} %bitcast.12, bf16[64,7168]{1,0:T(8,128)(2,1)S(1)} %copy-done.3), custom_call_target="tpu_custom_call" | custom-call | tf_op jit(solution)/shard_map/pallas_call | solution.py:69
  3.4 3.0 %collective-permute-start.2 = (bf16[40,7168]{1,0:T(8,128)(2,1)S(1)}, bf16[40,7168]{1,0:T(8,128)(2,1)S(1)}, u32[]{:S(2)}, u32[]{:S(2)}) collective-permute-start(bf16[40,7168]{1,0:T(8,128)(2,1)S(1)} %get-tuple-element.17), channel_id=1, source_target_pairs={{0,2},{2,0},{4,6},{6,4},{8,10},{10,8},{12,14},{14,12},{1,3},{3,1},... | collective-permute-start | bytes 1720328 | tf_op jit(solution)/shard_map/ppermute | solution.py:159
  6.5 1.6 %collective-permute-start.7 = (bf16[40,7168]{1,0:T(8,128)(2,1)S(1)}, bf16[40,7168]{1,0:T(8,128)(2,1)S(1)}, u32[]{:S(2)}, u32[]{:S(2)}) collective-permute-start(bf16[40,7168]{1,0:T(8,128)(2,1)S(1)} %get-tuple-element.20), channel_id=1, source_target_pairs={{0,4},{2,6},{4,8},{6,10},{8,12},{10,14},{12,0},{14,2},{1,5},{3,7},... | collective-permute-start | bytes 1720328 | tf_op jit(solution)/shard_map/ppermute | solution.py:154
  8.0 4.1 %constant_dynamic-slice_fusion = (bf16[256,3584]{1,0:T(8,128)(2,1)}, bf16[256,3584]{1,0:T(8,128)(2,1)}) fusion(bf16[256,7168]{1,0:T(8,128)(2,1)} %param.11, s32[]{:T(128)S(6)} %select_n.40, s32[]{:T(128)S(6)} %select_n.41), kind=kLoop, calls=%fused_computation.78 | loop fusion | bytes 7340040 | tf_op jit(solution)/shard_map/dynamic_slice | solution.py:191
  14.8 4.6 %collective-permute-done.2 = bf16[40,7168]{1,0:T(8,128)(2,1)S(1)} collective-permute-done((bf16[40,7168]{1,0:T(8,128)(2,1)S(1)}, bf16[40,7168]{1,0:T(8,128)(2,1)S(1)}, u32[]{:S(2)}, u32[]{:S(2)}) %collective-permute-start.2) | collective-permute-done | bytes 573472 | tf_op jit(solution)/shard_map/ppermute | solution.py:159
  19.4 4.3 %collective-permute-done.7 = bf16[40,7168]{1,0:T(8,128)(2,1)S(1)} collective-permute-done((bf16[40,7168]{1,0:T(8,128)(2,1)S(1)}, bf16[40,7168]{1,0:T(8,128)(2,1)S(1)}, u32[]{:S(2)}, u32[]{:S(2)}) %collective-permute-start.7) | collective-permute-done | bytes 573472 | tf_op jit(solution)/shard_map/ppermute | solution.py:154
  23.9 1.8 %collective-permute-start.14 = (bf16[40,7168]{1,0:T(8,128)(2,1)S(1)}, bf16[40,7168]{1,0:T(8,128)(2,1)S(1)}, u32[]{:S(2)}, u32[]{:S(2)}) collective-permute-start(bf16[40,7168]{1,0:T(8,128)(2,1)S(1)} %add_convert_fusion.9), channel_id=1, source_target_pairs={{0,12},{2,14},{4,0},{6,2},{8,4},{10,6},{12,8},{14,10},{1,13},{3,15... | collective-permute-start | bytes 1720328 | tf_op jit(solution)/shard_map/ppermute | solution.py:154
  27.4 2.0 %copy-done.1 = bf16[7168,256]{1,0:T(8,128)(2,1)S(1)} copy-done((bf16[7168,256]{1,0:T(8,128)(2,1)S(1)}, bf16[7168,256]{1,0:T(8,128)(2,1)}, u32[]{:S(2)}) %copy-start.1) | copy-done | bytes 3670040
  29.4 1.4 shard_map.65
  31.5 8.5 %collective-permute-done.9 = bf16[40,7168]{1,0:T(8,128)(2,1)S(1)} collective-permute-done((bf16[40,7168]{1,0:T(8,128)(2,1)S(1)}, bf16[40,7168]{1,0:T(8,128)(2,1)S(1)}, u32[]{:S(2)}, u32[]{:S(2)}) %collective-permute-start.9) | collective-permute-done | bytes 573472 | tf_op jit(solution)/shard_map/ppermute | solution.py:159
  42.1 1.4 shard_map.67
  45.0 1.7 %pad_maximum_fusion.down_ref = bf16[512,3584]{1,0:T(8,128)(2,1)S(1)} fusion(bf16[256,3584]{1,0:T(8,128)(2,1)} %collective-permute-done.5, bf16[256,3584]{1,0:T(8,128)(2,1)S(1)} %copy-done.6), kind=kLoop, calls=%fused_computation | loop fusion | flops 7340032 | bytes 7340032 | tf_op jit(solution)/shard_map/concatenate | solution.py:192
  48.2 7.8 %collective-permute-done.16 = bf16[40,7168]{1,0:T(8,128)(2,1)S(1)} collective-permute-done((bf16[40,7168]{1,0:T(8,128)(2,1)S(1)}, bf16[40,7168]{1,0:T(8,128)(2,1)S(1)}, u32[]{:S(2)}, u32[]{:S(2)}) %collective-permute-start.16) | collective-permute-done | bytes 573472 | tf_op jit(solution)/shard_map/ppermute | solution.py:159
  57.1 10.9 %collective-permute-done.12 = bf16[80,3584]{1,0:T(8,128)(2,1)S(1)} collective-permute-done((bf16[80,3584]{1,0:T(8,128)(2,1)S(1)}, bf16[80,3584]{1,0:T(8,128)(2,1)S(1)}, u32[]{:S(2)}, u32[]{:S(2)}) %collective-permute-start.12) | collective-permute-done | bytes 573472 | tf_op jit(solution)/shard_map/ppermute | solution.py:159
  72.3 2.0 %collective-permute-start.13 = (bf16[80,3584]{1,0:T(8,128)(2,1)S(1)}, bf16[80,3584]{1,0:T(8,128)(2,1)S(1)}, u32[]{:S(2)}, u32[]{:S(2)}) collective-permute-start(bf16[80,3584]{1,0:T(8,128)(2,1)S(1)} %add_convert_fusion.10), channel_id=1, source_target_pairs={{0,12},{2,14},{4,0},{6,2},{8,4},{10,6},{12,8},{14,10},{1,13},{3,15... | collective-permute-start | bytes 1720328 | tf_op jit(solution)/shard_map/ppermute | solution.py:154
  75.1 8.5 %collective-permute-done.23 = bf16[40,7168]{1,0:T(8,128)(2,1)S(1)} collective-permute-done((bf16[40,7168]{1,0:T(8,128)(2,1)S(1)}, bf16[40,7168]{1,0:T(8,128)(2,1)S(1)}, u32[]{:S(2)}, u32[]{:S(2)}) %collective-permute-start.23) | collective-permute-done | bytes 573472 | tf_op jit(solution)/shard_map/ppermute | solution.py:159
  84.7 3.2 %collective-permute-done.13 = bf16[80,3584]{1,0:T(8,128)(2,1)S(1)} collective-permute-done((bf16[80,3584]{1,0:T(8,128)(2,1)S(1)}, bf16[80,3584]{1,0:T(8,128)(2,1)S(1)}, u32[]{:S(2)}, u32[]{:S(2)}) %collective-permute-start.13) | collective-permute-done | bytes 573472 | tf_op jit(solution)/shard_map/ppermute | solution.py:154
  89.6 9.8 %collective-permute-done.19 = bf16[80,3584]{1,0:T(8,128)(2,1)S(1)} collective-permute-done((bf16[80,3584]{1,0:T(8,128)(2,1)S(1)}, bf16[80,3584]{1,0:T(8,128)(2,1)S(1)}, u32[]{:S(2)}, u32[]{:S(2)}) %collective-permute-start.19) | collective-permute-done | bytes 573472 | tf_op jit(solution)/shard_map/ppermute | solution.py:159
  101.5 1.4 collective-permute-start.6
  103.0 13.0 %collective-permute-done.20 = bf16[80,3584]{1,0:T(8,128)(2,1)S(1)} collective-permute-done((bf16[80,3584]{1,0:T(8,128)(2,1)S(1)}, bf16[80,3584]{1,0:T(8,128)(2,1)S(1)}, u32[]{:S(2)}, u32[]{:S(2)}) %collective-permute-start.20) | collective-permute-done | bytes 573472 | tf_op jit(solution)/shard_map/ppermute | solution.py:154
  116.7 1.8 %collective-permute-start.27 = (bf16[80,3584]{1,0:T(8,128)(2,1)S(1)}, bf16[80,3584]{1,0:T(8,128)(2,1)S(1)}, u32[]{:S(2)}, u32[]{:S(2)}) collective-permute-start(bf16[80,3584]{1,0:T(8,128)(2,1)S(1)} %add_convert_fusion), channel_id=1, source_target_pairs={{0,8},{2,10},{4,12},{6,14},{8,0},{10,2},{12,4},{14,6},{1,9},{3,11}... | collective-permute-start | bytes 1720328 | tf_op jit(solution)/shard_map/ppermute | solution.py:154
  118.5 9.1 %collective-permute-done.6 = bf16[80,3584]{1,0:T(8,128)(2,1)S(1)} collective-permute-done((bf16[80,3584]{1,0:T(8,128)(2,1)S(1)}, bf16[80,3584]{1,0:T(8,128)(2,1)S(1)}, u32[]{:S(2)}, u32[]{:S(2)}) %collective-permute-start.6) | collective-permute-done | bytes 573472 | tf_op jit(solution)/shard_map/ppermute | solution.py:159
  127.7 15.4 %collective-permute-done.27 = bf16[80,3584]{1,0:T(8,128)(2,1)S(1)} collective-permute-done((bf16[80,3584]{1,0:T(8,128)(2,1)S(1)}, bf16[80,3584]{1,0:T(8,128)(2,1)S(1)}, u32[]{:S(2)}, u32[]{:S(2)}) %collective-permute-start.27) | collective-permute-done | bytes 573472 | tf_op jit(solution)/shard_map/ppermute | solution.py:154
  144.6 1.8 %collective-permute-done.28 = bf16[64,3584]{1,0:T(8,128)(2,1)S(1)} collective-permute-done((bf16[64,3584]{1,0:T(8,128)(2,1)S(1)}, bf16[64,3584]{1,0:T(8,128)(2,1)S(1)}, u32[]{:S(2)}, u32[]{:S(2)}) %collective-permute-start.28) | collective-permute-done | bytes 458784 | tf_op jit(solution)/shard_map/ppermute | solution.py:162
  (111 shorter events, 26.1 us)
Async XLA Ops:
  3.4 16.0 %collective-permute-start.2 = (bf16[40,7168]{1,0:T(8,128)(2,1)S(1)}, bf16[40,7168]{1,0:T(8,128)(2,1)S(1)}, u32[]{:S(2)}, u32[]{:S(2)}) collective-permute-start(bf16[40,7168]{1,0:T(8,128)(2,1)S(1)} %get-tuple-element.17), channel_id=1, source_target_pairs={{0,2},{2,0},{4,6},{6,4},{8,10},{10,8},{12,14},{14,12},{1,3},{3,1},... | collective-permute-start | bytes 1720328 | tf_op jit(solution)/shard_map/ppermute | solution.py:159
  6.5 19.7 %collective-permute-start.1 = (bf16[40,7168]{1,0:T(8,128)(2,1)S(1)}, bf16[40,7168]{1,0:T(8,128)(2,1)}, u32[]{:S(2)}, u32[]{:S(2)}) collective-permute-start(bf16[40,7168]{1,0:T(8,128)(2,1)S(1)} %get-tuple-element.17), channel_id=1, source_target_pairs={{0,1},{1,0},{2,3},{3,2},{4,5},{5,4},{6,7},{7,6},{8,9},{9,8},{10,11... | collective-permute-start | bytes 1720328 | tf_op jit(solution)/shard_map/ppermute | solution.py:162
  6.5 17.2 %collective-permute-start.7 = (bf16[40,7168]{1,0:T(8,128)(2,1)S(1)}, bf16[40,7168]{1,0:T(8,128)(2,1)S(1)}, u32[]{:S(2)}, u32[]{:S(2)}) collective-permute-start(bf16[40,7168]{1,0:T(8,128)(2,1)S(1)} %get-tuple-element.20), channel_id=1, source_target_pairs={{0,4},{2,6},{4,8},{6,10},{8,12},{10,14},{12,0},{14,2},{1,5},{3,7},... | collective-permute-start | bytes 1720328 | tf_op jit(solution)/shard_map/ppermute | solution.py:154
  12.1 32.8 %collective-permute-start.5 = (bf16[256,3584]{1,0:T(8,128)(2,1)}, bf16[256,3584]{1,0:T(8,128)(2,1)}, u32[]{:S(2)}, u32[]{:S(2)}) collective-permute-start(bf16[256,3584]{1,0:T(8,128)(2,1)} %get-tuple-element.30), channel_id=1, source_target_pairs={{0,1},{1,0},{2,3},{3,2},{4,5},{5,4},{6,7},{7,6},{8,9},{9,8},{10,11... | collective-permute-start | bytes 5505032 | tf_op jit(solution)/shard_map/ppermute | solution.py:162
  19.4 6.7 %collective-permute-start.3 = (bf16[40,7168]{1,0:T(8,128)(2,1)S(1)}, bf16[40,7168]{1,0:T(8,128)(2,1)S(1)}, u32[]{:S(2)}, u32[]{:S(2)}) collective-permute-start(bf16[40,7168]{1,0:T(8,128)(2,1)S(1)} %collective-permute-done.2), channel_id=1, source_target_pairs={{0,1},{1,0},{2,3},{3,2},{4,5},{5,4},{6,7},{7,6},{8,9},{9,8},{10,11... | collective-permute-start | bytes 1720328 | tf_op jit(solution)/shard_map/ppermute | solution.py:162
  23.9 16.1 %collective-permute-start.14 = (bf16[40,7168]{1,0:T(8,128)(2,1)S(1)}, bf16[40,7168]{1,0:T(8,128)(2,1)S(1)}, u32[]{:S(2)}, u32[]{:S(2)}) collective-permute-start(bf16[40,7168]{1,0:T(8,128)(2,1)S(1)} %add_convert_fusion.9), channel_id=1, source_target_pairs={{0,12},{2,14},{4,0},{6,2},{8,4},{10,6},{12,8},{14,10},{1,13},{3,15... | collective-permute-start | bytes 1720328 | tf_op jit(solution)/shard_map/ppermute | solution.py:154
  25.7 14.3 %collective-permute-start.9 = (bf16[40,7168]{1,0:T(8,128)(2,1)S(1)}, bf16[40,7168]{1,0:T(8,128)(2,1)S(1)}, u32[]{:S(2)}, u32[]{:S(2)}) collective-permute-start(bf16[40,7168]{1,0:T(8,128)(2,1)S(1)} %collective-permute-done.7), channel_id=1, source_target_pairs={{0,2},{2,0},{4,6},{6,4},{8,10},{10,8},{12,14},{14,12},{1,3},{3,1},... | collective-permute-start | bytes 1720328 | tf_op jit(solution)/shard_map/ppermute | solution.py:159
  26.2 14.6 %collective-permute-start.8 = (bf16[40,7168]{1,0:T(8,128)(2,1)S(1)}, bf16[40,7168]{1,0:T(8,128)(2,1)S(1)}, u32[]{:S(2)}, u32[]{:S(2)}) collective-permute-start(bf16[40,7168]{1,0:T(8,128)(2,1)S(1)} %collective-permute-done.7), channel_id=1, source_target_pairs={{0,1},{1,0},{2,3},{3,2},{4,5},{5,4},{6,7},{7,6},{8,9},{9,8},{10,11... | collective-permute-start | bytes 1720328 | tf_op jit(solution)/shard_map/ppermute | solution.py:162
  30.9 9.3 %collective-permute-start.4 = (bf16[160,256]{1,0:T(8,128)(2,1)S(1)}, bf16[160,256]{1,0:T(8,128)(2,1)S(1)}, u32[]{:S(2)}, u32[]{:S(2)}) collective-permute-start(bf16[160,256]{1,0:T(8,128)(2,1)S(1)} %shard_map.65), channel_id=1, source_target_pairs={{0,1},{1,0},{2,3},{3,2},{4,5},{5,4},{6,7},{7,6},{8,9},{9,8},{10,11... | collective-permute-start | bytes 245768 | tf_op jit(solution)/shard_map/ppermute | solution.py:162
  40.1 28.4 %collective-permute-start.21 = (bf16[40,7168]{1,0:T(8,128)(2,1)S(1)}, bf16[40,7168]{1,0:T(8,128)(2,1)S(1)}, u32[]{:S(2)}, u32[]{:S(2)}) collective-permute-start(bf16[40,7168]{1,0:T(8,128)(2,1)S(1)} %add_convert_fusion.5), channel_id=1, source_target_pairs={{0,8},{2,10},{4,12},{6,14},{8,0},{10,2},{12,4},{14,6},{1,9},{3,11}... | collective-permute-start | bytes 1720328 | tf_op jit(solution)/shard_map/ppermute | solution.py:154
  40.2 15.8 %collective-permute-start.16 = (bf16[40,7168]{1,0:T(8,128)(2,1)S(1)}, bf16[40,7168]{1,0:T(8,128)(2,1)S(1)}, u32[]{:S(2)}, u32[]{:S(2)}) collective-permute-start(bf16[40,7168]{1,0:T(8,128)(2,1)S(1)} %collective-permute-done.14), channel_id=1, source_target_pairs={{0,2},{2,0},{4,6},{6,4},{8,10},{10,8},{12,14},{14,12},{1,3},{3,1},... | collective-permute-start | bytes 1720328 | tf_op jit(solution)/shard_map/ppermute | solution.py:159
  40.8 28.6 %collective-permute-start.15 = (bf16[40,7168]{1,0:T(8,128)(2,1)S(1)}, bf16[40,7168]{1,0:T(8,128)(2,1)S(1)}, u32[]{:S(2)}, u32[]{:S(2)}) collective-permute-start(bf16[40,7168]{1,0:T(8,128)(2,1)S(1)} %collective-permute-done.14), channel_id=1, source_target_pairs={{0,1},{1,0},{2,3},{3,2},{4,5},{5,4},{6,7},{7,6},{8,9},{9,8},{10,11... | collective-permute-start | bytes 1720328 | tf_op jit(solution)/shard_map/ppermute | solution.py:162
  47.5 20.4 %collective-permute-start.12 = (bf16[80,3584]{1,0:T(8,128)(2,1)S(1)}, bf16[80,3584]{1,0:T(8,128)(2,1)S(1)}, u32[]{:S(2)}, u32[]{:S(2)}) collective-permute-start(bf16[80,3584]{1,0:T(8,128)(2,1)S(1)} %get-tuple-element.22), channel_id=1, source_target_pairs={{0,2},{2,0},{4,6},{6,4},{8,10},{10,8},{12,14},{14,12},{1,3},{3,1},... | collective-permute-start | bytes 1720328 | tf_op jit(solution)/shard_map/ppermute | solution.py:159
  56.2 13.2 %collective-permute-start.17 = (bf16[40,7168]{1,0:T(8,128)(2,1)S(1)}, bf16[40,7168]{1,0:T(8,128)(2,1)S(1)}, u32[]{:S(2)}, u32[]{:S(2)}) collective-permute-start(bf16[40,7168]{1,0:T(8,128)(2,1)S(1)} %add_convert_fusion.8), channel_id=1, source_target_pairs={{0,1},{1,0},{2,3},{3,2},{4,5},{5,4},{6,7},{7,6},{8,9},{9,8},{10,11... | collective-permute-start | bytes 1720328 | tf_op jit(solution)/shard_map/ppermute | solution.py:162
  68.7 15.0 %collective-permute-start.23 = (bf16[40,7168]{1,0:T(8,128)(2,1)S(1)}, bf16[40,7168]{1,0:T(8,128)(2,1)S(1)}, u32[]{:S(2)}, u32[]{:S(2)}) collective-permute-start(bf16[40,7168]{1,0:T(8,128)(2,1)S(1)} %add_convert_fusion.4), channel_id=1, source_target_pairs={{0,2},{2,0},{4,6},{6,4},{8,10},{10,8},{12,14},{14,12},{1,3},{3,1},... | collective-permute-start | bytes 1720328 | tf_op jit(solution)/shard_map/ppermute | solution.py:159
  69.4 18.6 %collective-permute-start.22 = (bf16[40,7168]{1,0:T(8,128)(2,1)S(1)}, bf16[40,7168]{1,0:T(8,128)(2,1)S(1)}, u32[]{:S(2)}, u32[]{:S(2)}) collective-permute-start(bf16[40,7168]{1,0:T(8,128)(2,1)S(1)} %add_convert_fusion.4), channel_id=1, source_target_pairs={{0,1},{1,0},{2,3},{3,2},{4,5},{5,4},{6,7},{7,6},{8,9},{9,8},{10,11... | collective-permute-start | bytes 1720328 | tf_op jit(solution)/shard_map/ppermute | solution.py:162
  72.3 15.6 %collective-permute-start.13 = (bf16[80,3584]{1,0:T(8,128)(2,1)S(1)}, bf16[80,3584]{1,0:T(8,128)(2,1)S(1)}, u32[]{:S(2)}, u32[]{:S(2)}) collective-permute-start(bf16[80,3584]{1,0:T(8,128)(2,1)S(1)} %add_convert_fusion.10), channel_id=1, source_target_pairs={{0,12},{2,14},{4,0},{6,2},{8,4},{10,6},{12,8},{14,10},{1,13},{3,15... | collective-permute-start | bytes 1720328 | tf_op jit(solution)/shard_map/ppermute | solution.py:154
  84.0 15.4 %collective-permute-start.19 = (bf16[80,3584]{1,0:T(8,128)(2,1)S(1)}, bf16[80,3584]{1,0:T(8,128)(2,1)S(1)}, u32[]{:S(2)}, u32[]{:S(2)}) collective-permute-start(bf16[80,3584]{1,0:T(8,128)(2,1)S(1)} %add_convert_fusion.7), channel_id=1, source_target_pairs={{0,2},{2,0},{4,6},{6,4},{8,10},{10,8},{12,14},{14,12},{1,3},{3,1},... | collective-permute-start | bytes 1720328 | tf_op jit(solution)/shard_map/ppermute | solution.py:159
  89.5 10.1 %collective-permute-start.25 = (bf16[160,256]{1,0:T(8,128)(2,1)S(1)}, bf16[160,256]{1,0:T(8,128)(2,1)S(1)}, u32[]{:S(2)}, u32[]{:S(2)}) collective-permute-start(bf16[160,256]{1,0:T(8,128)(2,1)S(1)} %shard_map.71), channel_id=1, source_target_pairs={{0,1},{1,0},{2,3},{3,2},{4,5},{5,4},{6,7},{7,6},{8,9},{9,8},{10,11... | collective-permute-start | bytes 245768 | tf_op jit(solution)/shard_map/ppermute | solution.py:162
  99.6 16.4 %collective-permute-start.20 = (bf16[80,3584]{1,0:T(8,128)(2,1)S(1)}, bf16[80,3584]{1,0:T(8,128)(2,1)S(1)}, u32[]{:S(2)}, u32[]{:S(2)}) collective-permute-start(bf16[80,3584]{1,0:T(8,128)(2,1)S(1)} %add_convert_fusion.6), channel_id=1, source_target_pairs={{0,4},{2,6},{4,8},{6,10},{8,12},{10,14},{12,0},{14,2},{1,5},{3,7},... | collective-permute-start | bytes 1720328 | tf_op jit(solution)/shard_map/ppermute | solution.py:154
  100.6 15.9 %collective-permute-start.26 = (bf16[80,3584]{1,0:T(8,128)(2,1)S(1)}, bf16[80,3584]{1,0:T(8,128)(2,1)S(1)}, u32[]{:S(2)}, u32[]{:S(2)}) collective-permute-start(bf16[80,3584]{1,0:T(8,128)(2,1)S(1)} %add_convert_fusion.2), channel_id=1, source_target_pairs={{0,2},{2,0},{4,6},{6,4},{8,10},{10,8},{12,14},{14,12},{1,3},{3,1},... | collective-permute-start | bytes 1720328 | tf_op jit(solution)/shard_map/ppermute | solution.py:159
  101.4 26.2 %collective-permute-start = (bf16[128,320]{1,0:T(8,128)(2,1)S(1)}, bf16[128,320]{1,0:T(8,128)(2,1)S(1)}, u32[]{:S(2)}, u32[]{:S(2)}) collective-permute-start(bf16[128,320]{1,0:T(8,128)(2,1)S(1)} %pad_maximum_fusion.5), channel_id=1, source_target_pairs={{0,1},{1,0},{2,3},{3,2},{4,5},{5,4},{6,7},{7,6},{8,9},{9,8},{10,11... | collective-permute-start | bytes 245768 | tf_op jit(solution)/shard_map/ppermute | solution.py:162
  101.5 26.0 %collective-permute-start.6 = (bf16[80,3584]{1,0:T(8,128)(2,1)S(1)}, bf16[80,3584]{1,0:T(8,128)(2,1)S(1)}, u32[]{:S(2)}, u32[]{:S(2)}) collective-permute-start(bf16[80,3584]{1,0:T(8,128)(2,1)S(1)} %get-tuple-element.19), channel_id=1, source_target_pairs={{0,2},{2,0},{4,6},{6,4},{8,10},{10,8},{12,14},{14,12},{1,3},{3,1},... | collective-permute-start | bytes 1720328 | tf_op jit(solution)/shard_map/ppermute | solution.py:159
  116.7 26.4 %collective-permute-start.27 = (bf16[80,3584]{1,0:T(8,128)(2,1)S(1)}, bf16[80,3584]{1,0:T(8,128)(2,1)S(1)}, u32[]{:S(2)}, u32[]{:S(2)}) collective-permute-start(bf16[80,3584]{1,0:T(8,128)(2,1)S(1)} %add_convert_fusion), channel_id=1, source_target_pairs={{0,8},{2,10},{4,12},{6,14},{8,0},{10,2},{12,4},{14,6},{1,9},{3,11}... | collective-permute-start | bytes 1720328 | tf_op jit(solution)/shard_map/ppermute | solution.py:154
  (13 other events, 35.0 us)
